TPU v7x, 512 devices: a whole 4x4x16 slice. The times are simulated.
512 devices in a mesh: dp: 16 (over z_lo, core), ctx: 32 (over y, x, z_hi).
Axes of the slice: x: 4, y: 4, z: 16 (z_hi: 2, z_lo: 8; z = z_hi * 8 + z_lo), core: 2. Of those that a mesh axis runs over, the one named last changes fastest.
Arguments:
- normed: bfloat16 [65536, 8192], P(('dp', 'ctx')), may hold values from -24 to 24
- query: bfloat16 [65536, 512], P(('dp', 'ctx')), may hold values from -162 to 162
- key_value: bfloat16 [65536, 256], P(('dp', 'ctx')), may hold values from -6 to 6
- output_grad: bfloat16 [65536, 512], P(('dp', 'ctx')), may hold values from -6 to 6
- lengths: int32 [16, 16], P('dp'), may hold values from 1 to 1024, 4096 in all within a row
- advantage: float32 [16, 16], P('dp'), may hold values from -4 to 4
- span_plan: int32 [16, 32, 32], P('dp'), may hold values from 0 to 31, each once within a row
Outputs:
- query_grad: bfloat16 [65536, 512], P(('dp', 'ctx'))
- key_value_grad: bfloat16 [65536, 256], P(('dp', 'ctx'))
- weight_grad: bfloat16 [8192, 256], P(('ctx', 'dp'))
Inputs may be any that keep to these rules, and one draw needn't show every extreme that they name: Each row holds the lengths of the 16 documents of one group in order; they sum to 4096 and the longest is exactly 1024. span_plan[g, s, c] is the block of 4 rows, counted within the rows of device s of group g, that span c takes; for each g and s the entries over c are a permutation.
All inputs are finite; a program needn't handle non-finite values.
Results may differ from a plain program's by a relative error of at most 0.029.
Values may be sent and summed in bfloat16 or wider, within the bound.
A program may use at most 64 MiB of HBM per device.

v0:
```python
import jax
import jax.numpy as jnp
from jax import lax
from jax.sharding import PartitionSpec as P

NEG_FILL = -1e30
KEY_BLOCK = 512


def doc_index(lengths, positions):
    doc_ends = jnp.cumsum(lengths)
    return jnp.sum((positions[:, None] >= doc_ends[None, :]).astype(jnp.int32), axis=1)


def per_token(doc_table, token_docs):
    matches = token_docs[:, None] == jnp.arange(doc_table.shape[0], dtype=jnp.int32)[None, :]
    return jnp.sum(jnp.where(matches, doc_table[None, :], jnp.zeros((), doc_table.dtype)), axis=1)


def over_blocks(block_step, totals, shard_rows, first_row):
    piece_rows = shard_rows.shape[0]
    block_len = min(KEY_BLOCK, piece_rows)

    def inner(block_number, state):
        key_block = lax.dynamic_slice_in_dim(shard_rows, block_number * block_len, block_len, 0)
        return block_step(state, key_block, first_row + block_number * block_len)

    return lax.fori_loop(0, piece_rows // block_len, inner, totals)


def local(normed, query, key_value, output_grad, lengths, advantage, span_plan):
    tok_rows = query.shape[0]
    ctx_count = lax.axis_size("ctx")
    rows_per_block = tok_rows // ctx_count
    context = tok_rows * ctx_count
    head_dim = key_value.shape[1] // 2
    heads = query.shape[1] // head_dim
    score_scale = head_dim ** (-0.5)
    own_index = lax.axis_index("ctx")
    doc_lengths = lengths[0]
    route_table = span_plan[0]
    all_pos = jnp.arange(context, dtype=jnp.int32)
    all_docs = doc_index(doc_lengths, all_pos)
    own_docs = lax.dynamic_slice_in_dim(all_docs, own_index * tok_rows, tok_rows, 0)
    weighted = (
        per_token(advantage[0], own_docs)[:, None] * output_grad.astype(jnp.float32)
    ).astype(jnp.bfloat16)
    chosen_blocks = route_table[own_index]

    def to_blocks(row_data):
        row_blocks = row_data.reshape(ctx_count, rows_per_block, row_data.shape[1])
        return jnp.take(row_blocks, chosen_blocks, axis=0)

    recv_query, recv_grad = (
        lax.all_to_all(to_blocks(query), "ctx", split_axis=0, concat_axis=0, tiled=True),
        lax.all_to_all(to_blocks(weighted), "ctx", split_axis=0, concat_axis=0, tiled=True),
    )
    q_rows = recv_query.reshape(tok_rows, heads, head_dim)
    o_rows = recv_grad.reshape(tok_rows, heads, head_dim)
    span_pos = (
        jnp.arange(ctx_count, dtype=jnp.int32)[:, None] * tok_rows
        + route_table[:, own_index][:, None] * rows_per_block
        + jnp.arange(rows_per_block, dtype=jnp.int32)[None, :]
    ).reshape(tok_rows)
    span_docs = doc_index(doc_lengths, span_pos)
    x_slices = lax.all_to_all(normed, "ctx", split_axis=1, concat_axis=0, tiled=True)

    def block_scores(key_block, first_row):
        block_len = key_block.shape[0]
        key_part = key_block[:, :head_dim]
        value_part = key_block[:, head_dim:]
        key_pos = first_row + jnp.arange(block_len, dtype=jnp.int32)
        key_docs = lax.dynamic_slice_in_dim(all_docs, first_row, block_len, 0)
        visible = (span_docs[:, None] == key_docs[None, :]) & (
            span_pos[:, None] >= key_pos[None, :]
        )
        scores = (
            jnp.einsum("qhe,ke->hqk", q_rows, key_part, preferred_element_type=jnp.float32)
            * score_scale
        )
        scores = jnp.where(visible[None], scores, NEG_FILL)
        grad_prob = jnp.einsum(
            "qhe,ke->hqk", o_rows, value_part, preferred_element_type=jnp.float32
        )
        return (scores, grad_prob, visible, key_part)

    def first_step(totals, key_block, first_row):
        running_max, running_sum, running_dot = totals
        scores, grad_prob, visible, key_part = block_scores(key_block, first_row)
        new_max = jnp.maximum(running_max, jnp.max(scores, axis=-1))
        rescale = jnp.exp(running_max - new_max)
        weights_exp = jnp.where(visible[None], jnp.exp(scores - new_max[..., None]), 0.0)
        return (
            new_max,
            running_sum * rescale + jnp.sum(weights_exp, axis=-1),
            running_dot * rescale + jnp.sum(weights_exp * grad_prob, axis=-1),
        )

    stat_shape = (heads, tok_rows)
    first_init = (
        jnp.full(stat_shape, NEG_FILL, jnp.float32),
        jnp.zeros(stat_shape, jnp.float32),
        jnp.zeros(stat_shape, jnp.float32),
    )
    kv_all = lax.all_gather(key_value, "ctx", axis=0, tiled=True)
    stats = over_blocks(first_step, first_init, kv_all, 0)
    log_total = stats[0] + jnp.log(stats[1])
    row_dot = stats[2] / stats[1]

    def second_step(totals, key_block, first_row):
        query_acc, partial_grads = totals
        scores, grad_prob, visible, key_part = block_scores(key_block, first_row)
        prob_full = jnp.where(visible[None], jnp.exp(scores - log_total[..., None]), 0.0)
        grad_score = (prob_full * (grad_prob - row_dot[..., None])).astype(jnp.bfloat16)
        prob_low = prob_full.astype(jnp.bfloat16)
        query_acc = query_acc + jnp.einsum(
            "hqk,ke->qhe", grad_score, key_part, preferred_element_type=jnp.float32
        )
        key_grad = (
            jnp.einsum("hqk,qhe->ke", grad_score, q_rows, preferred_element_type=jnp.float32)
            * score_scale
        )
        value_grad = jnp.einsum("hqk,qhe->ke", prob_low, o_rows, preferred_element_type=jnp.float32)
        block_grads = jnp.concatenate([key_grad, value_grad], axis=1)
        partial_grads = lax.dynamic_update_slice_in_dim(partial_grads, block_grads, first_row, 0)
        return (query_acc, partial_grads)

    second_init = (
        jnp.zeros((tok_rows, heads, head_dim), jnp.float32),
        jnp.zeros((context, 2 * head_dim), jnp.float32),
    )
    query_acc, partial_grads = over_blocks(second_step, second_init, kv_all, 0)
    query_grad = (query_acc * score_scale).reshape(tok_rows, heads * head_dim).astype(jnp.bfloat16)
    key_value_grad = lax.psum_scatter(
        partial_grads.astype(jnp.bfloat16), "ctx", scatter_dimension=0, tiled=True
    )
    weight_term = jnp.einsum(
        "td,tc->dc",
        x_slices,
        lax.all_gather(key_value_grad, "ctx", axis=0, tiled=True),
        preferred_element_type=jnp.float32,
    )
    total_tokens = context * lax.axis_size("dp")
    weight_grad = (
        lax.psum_scatter(weight_term, "dp", scatter_dimension=0, tiled=True)
        * total_tokens ** (-0.5)
    ).astype(jnp.bfloat16)
    return (query_grad, key_value_grad, weight_grad)


def solution(mesh):
    return jax.shard_map(
        local,
        mesh=mesh,
        in_specs=(
            P(("dp", "ctx"), None),
            P(("dp", "ctx"), None),
            P(("dp", "ctx"), None),
            P(("dp", "ctx"), None),
            P("dp", None),
            P("dp", None),
            P("dp", None, None),
        ),
        out_specs=(P(("dp", "ctx"), None), P(("dp", "ctx"), None), P(("ctx", "dp"), None)),
        check_vma=False,
    )
```

profile of v0, /device:TPU:1, one launch (start us, length us, event | category | flops | bytes accessed | tf_op | source)
XLA Modules:
  0.0 880.6 jit_solution(9818401318777363053)
XLA Ops:
  14.7 21.1 %all-to-all-start = ((bf16[32,4,512]{2,1,0:T(4,128)(2,1)}), bf16[32,4,512]{2,1,0:T(4,128)(2,1)S(1)}, u32[]{:S(2)}, u32[]{:S(2)}) async-start(bf16[32,4,512]{2,1,0:T(4,128)(2,1)} %get-tuple-element.600), calls=%async_computation | async-start | bytes 262144 | tf_op jit(solution)/shard_map/all_to_all | solution.py:55
  36.1 16.2 %all-to-all-done = bf16[32,4,512]{2,1,0:T(4,128)(2,1)S(1)} async-done(((bf16[32,4,512]{2,1,0:T(4,128)(2,1)}), bf16[32,4,512]{2,1,0:T(4,128)(2,1)S(1)}, u32[]{:S(2)}, u32[]{:S(2)}) %all-to-all-start) | async-done | bytes 131104 | tf_op jit(solution)/shard_map/all_to_all | solution.py:55
  52.3 3.9 all-to-all-start.1
  56.7 15.8 %all-to-all-done.1 = bf16[32,4,512]{2,1,0:T(4,128)(2,1)S(1)} async-done(((bf16[32,4,512]{2,1,0:T(4,128)(2,1)}), bf16[32,4,512]{2,1,0:T(4,128)(2,1)S(1)}, u32[]{:S(2)}, u32[]{:S(2)}) %all-to-all-start.1) | async-done | bytes 131104 | tf_op jit(solution)/shard_map/all_to_all | solution.py:56
  72.7 79.4 %all-gather.3.cloned.1.call-done = bf16[4096,256]{1,0:T(8,128)(2,1)} async-done(((bf16[128,256]{1,0:T(8,128)(2,1)}), bf16[4096,256]{1,0:T(8,128)(2,1)}) %all-gather.3.cloned.1.call-update) | async-done | bytes 2097168 | tf_op jit(solution)/shard_map/all_gather | solution.py:105
  152.2 26.0 %while.34 = (s32[]{:T(128)}, f32[4,128]{1,0:T(4,128)S(1)}, f32[4,128]{1,0:T(4,128)S(1)}, f32[4,128]{1,0:T(4,128)S(1)}, s32[128]{0:T(128)S(1)}, /*index=5*/s32[40...) while((s32[]{:T(128)}, f32[4,128]{1,0:T(4,128)S(1)}, ...), condition=%wide.region_8.10_spmd.clone, body=%wide.region_4.9_spmd.clone.sunk | while | flops 137040000 | bytes 3982190 | solution.py:28
  152.6 1.2 fusion.56
  153.9 1.3 fusion.57
  155.9 1.2 fusion.56
  157.1 1.3 fusion.57
  159.1 1.2 fusion.56
  160.4 1.3 fusion.57
  162.4 1.2 fusion.56
  163.6 1.3 fusion.57
  165.6 1.2 fusion.56
  166.9 1.3 fusion.57
  168.9 1.2 fusion.56
  170.1 1.3 fusion.57
  172.1 1.2 fusion.56
  173.4 1.3 fusion.57
  175.4 1.2 fusion.56
  176.6 1.3 fusion.57
  178.2 1.5 broadcast_in_dim.144.clone
  179.6 45.9 %while.35 = (s32[]{:T(128)}, f32[128,4,128]{0,2,1:T(8,128)S(1)}, bf16[4096,256]{1,0:T(8,128)(2,1)}, bf16[4096,256]{1,0:T(8,128)(2,1)}, s32[128]{0:T(128)S(1)}, /...) while((s32[]{:T(128)}, f32[128,4,128]{0,2,1:T(8,128)S(1)}, ...), condition=%wide.region_10.12_spmd.clone, body=%wide.region_9.11_spmd.clone.sunk | while | flops 338625152 | bytes 8143741 | solution.py:28
  180.1 1.3 fusion.67
  182.6 1.2 fusion.69
  185.8 1.3 fusion.67
  188.4 1.2 fusion.69
  191.6 1.3 fusion.67
  194.1 1.2 fusion.69
  197.3 1.3 fusion.67
  199.8 1.2 fusion.69
  203.1 1.3 fusion.67
  205.6 1.2 fusion.69
  208.8 1.3 fusion.67
  211.3 1.2 fusion.69
  214.6 1.3 fusion.67
  217.1 1.2 fusion.69
  220.3 1.3 fusion.67
  222.8 1.2 fusion.69
  225.6 1.6 copy-done
  227.2 2.4 copy.81
  229.6 4.8 all-to-all-start.2
  234.4 366.7 %reduce-scatter.5.cloned.1.call-done = bf16[128,256]{1,0:T(8,128)(2,1)} async-done(((bf16[4096,256]{1,0:T(8,128)(2,1)}), bf16[128,256]{1,0:T(8,128)(2,1)}) %reduce-scatter.5.cloned.1.call-update) | async-done | bytes 65552 | tf_op jit(solution)/shard_map/reduce_scatter | solution.py:134
  601.2 3.3 copy.82
  604.5 176.8 %all-gather.5.cloned.1.call-done = bf16[4096,256]{1,0:T(8,128)(2,1)} async-done(((bf16[128,256]{1,0:T(8,128)(2,1)}), bf16[4096,256]{1,0:T(8,128)(2,1)}) %all-gather.5.cloned.1.call-update) | async-done | bytes 2097168 | tf_op jit(solution)/shard_map/all_gather | solution.py:140
  781.3 2.3 convolution_bitcast_fusion.5
  785.3 87.2 %reduce-scatter.7.cloned.1.call-done = f32[16,256]{1,0:T(8,128)} async-done(((f32[256,256]{1,0:T(8,128)}), f32[16,256]{1,0:T(8,128)}) %reduce-scatter.7.cloned.1.call-update) | async-done | bytes 16400
  (208 shorter events, 42.5 us)
Async XLA Ops:
  7.2 28.7 %copy-start.1 = (s32[1,32,32]{2,1,0:T(8,128)S(1)}, s32[1,32,32]{2,1,0:T(8,128)}, u32[]{:S(2)}) copy-start(s32[1,32,32]{2,1,0:T(8,128)} %param.19) | copy-start | bytes 12292
  7.2 145.0 %all-gather.3.cloned.1.call-start = ((), (), s32[]{:S(2)}) async-start(), calls=%async_computation.5 | async-start | bytes 2162688 | tf_op jit(solution)/shard_map/all_gather | solution.py:105
  14.7 37.6 %all-to-all-start = ((bf16[32,4,512]{2,1,0:T(4,128)(2,1)}), bf16[32,4,512]{2,1,0:T(4,128)(2,1)S(1)}, u32[]{:S(2)}, u32[]{:S(2)}) async-start(bf16[32,4,512]{2,1,0:T(4,128)(2,1)} %get-tuple-element.600), calls=%async_computation | async-start | bytes 262144 | tf_op jit(solution)/shard_map/all_to_all | solution.py:55
  52.3 20.2 %all-to-all-start.1 = ((bf16[32,4,512]{2,1,0:T(4,128)(2,1)}), bf16[32,4,512]{2,1,0:T(4,128)(2,1)S(1)}, u32[]{:S(2)}, u32[]{:S(2)}) async-start(bf16[32,4,512]{2,1,0:T(4,128)(2,1)} %get-tuple-element.599), calls=%async_computation.1 | async-start | bytes 262144 | tf_op jit(solution)/shard_map/all_to_all | solution.py:56
  56.2 545.0 %reduce-scatter.5.cloned.1.call-start = ((), (), s32[]{:S(2)}) async-start(), calls=%async_computation.6 | async-start | bytes 2162688 | tf_op jit(solution)/shard_map/reduce_scatter | solution.py:134
  225.6 1.6 copy-start
  229.6 371.6 %all-to-all-start.2 = ((bf16[128,32,256]{0,2,1:T(8,128)(2,1)}), bf16[128,32,256]{0,2,1:T(8,128)(2,1)}, u32[]{:S(2)}, u32[]{:S(2)}) async-start(bf16[128,32,256]{0,2,1:T(8,128)(2,1)} %bitcast.4), calls=%async_computation.3 | async-start | bytes 4194304 | tf_op jit(solution)/shard_map/all_to_all | solution.py:66
  234.4 546.9 %all-gather.5.cloned.1.call-start = ((), (), s32[]{:S(2)}) async-start(), calls=%async_computation.7 | async-start | bytes 2162688 | tf_op jit(solution)/shard_map/all_gather | solution.py:140
  601.2 271.4 %reduce-scatter.7.cloned.1.call-start = ((), (), s32[]{:S(2)}) async-start(), calls=%async_computation.8 | async-start | bytes 278528
Sparse Core Ops, SparseCore 0:
  12.3 139.7 all-gather.2
  225.7 375.3 reduce-scatter.4
  606.8 174.4 all-gather.4
  784.6 87.8 reduce-scatter.6
where the time goes:
time: 889 us; the launch traced here: 881 us
  waiting for transfers between devices  743 us (84%)
  matrix products  56.6 us (6%)
  starting transfers between devices  29.9 us (3%)
  local copies, waits for them, and re-layouts  25.4 us (3%)
  between operations  14 us (2%)
  other arithmetic  10.5 us (1%)
    reduce_scatter x1, waiting for transfers between devices, local(): lax.psum_scatter(partial_grads.astype(jnp.bfloat16), 'ctx', scatter_dimen...  367 us
    all_gather x1, waiting for transfers between devices, local(): lax.all_gather(key_value_grad, 'ctx', axis=0, tiled=True)  177 us
    unnamed x5, waiting for transfers between devices  88 us
    all_gather x1, waiting for transfers between devices, local(): kv_all = lax.all_gather(key_value, 'ctx', axis=0, tiled=True)  79.4 us
    all_to_all x1, starting transfers between devices, local(): lax.all_to_all(to_blocks(query), 'ctx', split_axis=0, concat_axis=0, tile...  21.1 us
    dot_general x16, matrix products, block_scores(): jnp.einsum('qhe,ke->hqk', q_rows, key_part, preferred_element_type=jnp.fl...  20.1 us
    dot_general x16, matrix products, block_scores(): jnp.einsum('qhe,ke->hqk', o_rows, value_part, preferred_element_type=jnp....  19.7 us
  transfers between devices with their start and end apart: 7, of which 6 were waited for; matrix products, arithmetic and copies ran while one was open for 2% of the time, Pallas kernels for 0%

commit v1 on v0

v1 whole, which is shorter than its diff:
```python
import jax
import jax.numpy as jnp
from jax import lax
from jax.experimental import pallas as pl
from jax.experimental.pallas import tpu as pltpu
from jax.sharding import PartitionSpec as P

NEG_FILL = -1e30
MESH = pl.DeviceIdType.MESH
T = 128
HQ = 4
HD = 128
SEEN = 5
FEAT = 512
SCALE = HD**-0.5
FIRST = 7


def dot_nt(a, b):
    return lax.dot_general(a, b, (((1,), (1,)), ((), ())), preferred_element_type=jnp.float32)


def dot_nn(a, b):
    return lax.dot_general(a, b, (((1,), (0,)), ((), ())), preferred_element_type=jnp.float32)


def kernel(normed, query, kv, og, lengths, advantage, plan, qg_out, kvg_out, wg_out,
           q_in, og_in, q_st, o_st, kvb, k_t, bias, p_st, ds_st, onehot, part, got, own_far, far_sum, far_got,
           q_send, q_recv, x_got, x_t, g_all, w_acc, w_pair, w_pair_got, w_z, w_z_got,
           loc_sem, kz_s, kz_r, kp_s, kp_r, kf_s, kf_r, x_s, x_r, d_s, d_r, dz_s, dz_r, qa_s, qa_r, g_s, g_r, pr_s, pr_r, z_s, z_r):
    d = lax.axis_index("dp")
    c = lax.axis_index("ctx")
    j, p = c // 2, c % 2
    z_lo, core = d // 2, d % 2
    z = p * 8 + z_lo

    def plane(offset):
        return (d, lax.rem(j + offset, 16) * 2 + p)

    partner = (d, j * 2 + (1 - p))
    twin = (z_lo * 2 + (1 - core), c)

    def along_z(offset):
        there = lax.rem(z + offset, 16)
        return (lax.rem(there, 8) * 2 + core, j * 2 + there // 8)

    def remote(src, dst, send, recv, where):
        return pltpu.make_async_remote_copy(src_ref=src, dst_ref=dst, send_sem=send, recv_sem=recv,
                                            device_id=where, device_id_type=MESH)

    loads = [
        pltpu.make_async_copy(query, q_in, loc_sem.at[0]),
        pltpu.make_async_copy(og, og_in, loc_sem.at[1]),
        pltpu.make_async_copy(kv, kvb.at[0], loc_sem.at[2]),
        pltpu.make_async_copy(normed.at[:, pl.ds(pl.multiple_of(j * FEAT, FEAT), FEAT)], x_got.at[j], loc_sem.at[3]),
    ]
    for cp in loads:
        cp.start()

    barrier = pltpu.get_barrier_semaphore()

    def greet_ctx(o, carry):
        pl.semaphore_signal(barrier, inc=1, device_id=(d, lax.rem(c + o, 32)), device_id_type=MESH)
        return carry

    def greet_z(o, carry):
        pl.semaphore_signal(barrier, inc=1, device_id=along_z(o), device_id_type=MESH)
        return carry

    lax.fori_loop(1, 32, greet_ctx, 0)
    lax.fori_loop(1, 8, greet_z, 0)
    lax.fori_loop(9, 16, greet_z, 0)
    pl.semaphore_signal(barrier, inc=1, device_id=twin, device_id_type=MESH)
    pl.semaphore_wait(barrier, 46)

    halves = [pl.ds(0, HD), pl.ds(HD, HD)]
    kz = [remote(kv.at[:, half], kvb.at[SEEN, :, half], kz_s.at[i], kz_r.at[i], partner) for i, half in enumerate(halves)]
    for cp in kz:
        cp.start()
    kp = [remote(kv, kvb.at[o], kp_s.at[o - 1], kp_r.at[o - 1], plane(o)) for o in range(1, SEEN)]
    for cp in kp:
        cp.start()

    def x_copy(o):
        there = lax.rem(j + o, 16)
        return remote(normed.at[:, pl.ds(pl.multiple_of(there * FEAT, FEAT), FEAT)], x_got.at[j],
                      x_s.at[o - 1], x_r.at[o - 1], plane(o))

    def x_start(o, carry):
        x_copy(o).start()
        return carry

    lax.fori_loop(1, FIRST + 1, x_start, 0)

    lanes = lax.broadcasted_iota(jnp.int32, (1, T), 1)
    rows = lax.broadcasted_iota(jnp.int32, (T, HD), 0)
    pos_lane = c * T + lanes
    pos_row = c * T + rows
    start_lane = jnp.zeros((1, T), jnp.int32)
    adv_row = jnp.zeros((T, HD), jnp.float32)
    end = jnp.int32(0)
    for i in range(16):
        begin = end
        end = end + lengths[0, i]
        start_lane = jnp.where(pos_lane >= begin, begin, start_lane)
        adv_row = jnp.where(pos_row >= begin, advantage[0, i], adv_row)
    key_rows = lax.broadcasted_iota(jnp.int32, (T, T), 0)
    for rel in range(2):
        for o in range(SEEN):
            key_plane = p if rel == 0 else 1 - p
            base = ((j - o) * 2 + key_plane) * T
            seen = (key_rows >= start_lane - base) & (key_rows <= pos_lane - base)
            bias[pl.ds((rel * SEEN + o) * T, T), :] = jnp.where(seen, 0.0, NEG_FILL)

    plan_row = plan[pl.ds(c, 1), :]
    out_row = lax.broadcasted_iota(jnp.int32, (4 * T, 32), 0)
    span_no = lax.broadcasted_iota(jnp.int32, (4 * T, 32), 1)
    block = jnp.sum(jnp.where(out_row // 16 == span_no, jnp.broadcast_to(plan_row, (4 * T, 32)), 0), axis=1, keepdims=True)
    row_no = lax.broadcasted_iota(jnp.int32, (4 * T, 1), 0)
    source = (row_no // 4 % 4) * T + block * 4 + row_no % 4
    for h in range(HQ):
        col_no = lax.broadcasted_iota(jnp.int32, (4 * T, T), 1) + h * T
        onehot[:, pl.ds(h * T, T)] = jnp.where(col_no == source, 1.0, 0.0).astype(jnp.bfloat16)

    loads[0].wait()
    loads[1].wait()
    for h in range(HQ):
        cols = pl.ds(h * HD, HD)
        q_st[pl.ds(h * T, T), :] = q_in[:, cols]
        o_st[pl.ds(h * T, T), :] = (adv_row * og_in[:, cols].astype(jnp.float32)).astype(jnp.bfloat16)

    kf = []
    for i, half in enumerate(halves):
        kz[i].wait_recv()
        for o in range(1, SEEN):
            cp = remote(kvb.at[SEEN, :, half], kvb.at[SEEN + o, :, half], kf_s.at[i * 4 + o - 1], kf_r.at[i * 4 + o - 1], plane(o))
            cp.start()
            kf.append(cp)
    loads[2].wait()
    for cp in kp:
        cp.wait_recv()
    for cp in kf:
        cp.wait_recv()

    n_keys = 2 * SEEN * T
    keys = kvb[:, :, :HD].reshape(n_keys, HD)
    values = kvb[:, :, HD:].reshape(n_keys, HD)
    for s in range(2 * SEEN):
        k_t[:, pl.ds(s * T, T)] = kvb[s, :, :HD].T
    for h in range(HQ):
        heads = pl.ds(h * T, T)
        scores = dot_nt(keys, q_st[heads, :]) * SCALE + bias[...]
        top = jnp.max(scores, axis=0, keepdims=True)
        weights = jnp.exp(scores - top)
        probs = weights * (1.0 / jnp.sum(weights, axis=0, keepdims=True))
        grad_prob = dot_nt(values, o_st[heads, :])
        row_dot = jnp.sum(probs * grad_prob, axis=0, keepdims=True)
        ds_st[:, heads] = (probs * (grad_prob - row_dot)).astype(jnp.bfloat16)
        p_st[:, heads] = probs.astype(jnp.bfloat16)

    half_rows = SEEN * T

    def grads(rel):
        at = pl.ds(rel * half_rows, half_rows)
        dk = dot_nn(ds_st[at, :], q_st[...]) * SCALE
        dv = dot_nn(p_st[at, :], o_st[...])
        return jnp.concatenate([dk, dv], axis=1)

    sent = []
    for rel in (1, 0):
        terms = grads(rel)
        own_far[rel] = terms[:T]
        part[pl.ds(rel * 4, 4)] = terms[T:].astype(jnp.bfloat16).reshape(SEEN - 1, T, 2 * HD)
        for o in range(1, SEEN):
            i = rel * 4 + o - 1
            cp = remote(part.at[i], got.at[i], d_s.at[i], d_r.at[i], plane(16 - o))
            cp.start()
            sent.append((rel, cp))

    q_grad_t = (dot_nn(k_t[...], ds_st[...]) * SCALE).astype(jnp.bfloat16)
    q_send[...] = dot_nt(onehot[...], q_grad_t).astype(jnp.bfloat16).reshape(32, 16, HD)
    q_recv[c] = q_send[c]

    def terms_sum(rel):
        for r, cp in sent:
            if r == rel:
                cp.wait_recv()
        total = own_far[rel]
        for o in range(SEEN - 1):
            total = total + got[rel * 4 + o].astype(jnp.float32)
        return total

    far_sum[...] = terms_sum(1).astype(jnp.bfloat16)
    dz = remote(far_sum, far_got, dz_s, dz_r, partner)
    dz.start()

    lax.fori_loop(FIRST + 1, 16, x_start, 0)

    def q_copy(o):
        there = lax.rem(c + o, 32)
        return remote(q_send.at[there], q_recv.at[c], qa_s.at[o - 1], qa_r.at[o - 1], (d, there))

    def q_start(o, carry):
        q_copy(o).start()
        return carry

    lax.fori_loop(1, 32, q_start, 0)

    near = terms_sum(0)

    loads[3].wait()

    def turn(b):
        x_t[:, pl.ds(pl.multiple_of(b * T, T), T)] = x_got[b].T

    turn(j)

    def x_take(o, carry):
        x_copy(o).wait_recv()
        turn(lax.rem(j + 16 - o, 16))
        return carry

    lax.fori_loop(1, FIRST + 1, x_take, 0)

    dz.wait_recv()
    kvg = (near + far_got[...].astype(jnp.float32)).astype(jnp.bfloat16)
    g_all[j] = kvg

    def g_copy(o):
        return remote(g_all.at[j], g_all.at[j], g_s.at[o - 1], g_r.at[o - 1], plane(o))

    def g_start(o, carry):
        g_copy(o).start()
        return carry

    lax.fori_loop(1, 16, g_start, 0)
    kvg_out[...] = kvg

    lax.fori_loop(FIRST + 1, 16, x_take, 0)

    def g_take(o, carry):
        g_copy(o).wait_recv()
        return carry

    lax.fori_loop(1, 16, g_take, 0)

    w_acc[...] = dot_nn(x_t[...], g_all[...].reshape(16 * T, 2 * HD)).reshape(16, 2, 16, 2 * HD)
    w_pair[...] = w_acc[:, 1 - core].astype(jnp.bfloat16)
    pair = remote(w_pair, w_pair_got, pr_s, pr_r, twin)
    pair.start()
    pair.wait_recv()
    w_z[...] = (w_acc[:, core] + w_pair_got[...].astype(jnp.float32)).astype(jnp.bfloat16)
    w_z_got[z] = w_z[z]

    def z_copy(o):
        return remote(w_z.at[lax.rem(z + o, 16)], w_z_got.at[z], z_s.at[o - 1], z_r.at[o - 1], along_z(o))

    def z_start(o, carry):
        z_copy(o).start()
        return carry

    lax.fori_loop(1, 16, z_start, 0)

    def q_take(o, carry):
        q_copy(o).wait_recv()
        return carry

    lax.fori_loop(1, 32, q_take, 0)
    arrived = q_recv[...].reshape(4 * T, HD)
    tok = lax.broadcasted_iota(jnp.int32, (T, 4 * T), 0)
    place = lax.broadcasted_iota(jnp.int32, (T, 4 * T), 1)
    for h in range(HQ):
        pick = jnp.where(place == tok // 4 * 16 + h * 4 + tok % 4, 1.0, 0.0).astype(jnp.bfloat16)
        qg_out[:, pl.ds(h * HD, HD)] = dot_nn(pick, arrived).astype(jnp.bfloat16)

    def z_take(o, carry):
        z_copy(o).wait_recv()
        return carry

    lax.fori_loop(1, 16, z_take, 0)
    total = jnp.sum(w_z_got[...].astype(jnp.float32), axis=0)
    wg_out[...] = (total * (1.0 / 256.0)).astype(jnp.bfloat16)

    for cp in kz + kp + kf + [cp for _, cp in sent] + [dz, pair]:
        cp.wait_send()

    def plane_sent(o, carry):
        x_copy(o).wait_send()
        g_copy(o).wait_send()
        z_copy(o).wait_send()
        return carry

    lax.fori_loop(1, 16, plane_sent, 0)

    def q_sent(o, carry):
        q_copy(o).wait_send()
        return carry

    lax.fori_loop(1, 32, q_sent, 0)


def local(normed, query, key_value, output_grad, lengths, advantage, span_plan):
    bf16, f32 = jnp.bfloat16, jnp.float32
    n_keys = 2 * SEEN * T
    dma = pltpu.SemaphoreType.DMA
    any_space = pl.BlockSpec(memory_space=pl.ANY)
    vmem = pl.BlockSpec(memory_space=pltpu.VMEM)
    smem = pl.BlockSpec(memory_space=pltpu.SMEM)
    return pl.pallas_call(
        kernel,
        out_shape=(
            jax.ShapeDtypeStruct((T, HQ * HD), bf16),
            jax.ShapeDtypeStruct((T, 2 * HD), bf16),
            jax.ShapeDtypeStruct((16, 2 * HD), bf16),
        ),
        in_specs=[any_space, any_space, any_space, any_space, smem, smem, vmem],
        out_specs=(vmem, vmem, vmem),
        scratch_shapes=[
            pltpu.VMEM((T, HQ * HD), bf16),
            pltpu.VMEM((T, HQ * HD), bf16),
            pltpu.VMEM((HQ * T, HD), bf16),
            pltpu.VMEM((HQ * T, HD), bf16),
            pltpu.VMEM((2 * SEEN, T, 2 * HD), bf16),
            pltpu.VMEM((HD, n_keys), bf16),
            pltpu.VMEM((n_keys, T), f32),
            pltpu.VMEM((n_keys, HQ * T), bf16),
            pltpu.VMEM((n_keys, HQ * T), bf16),
            pltpu.VMEM((HQ * T, HQ * T), bf16),
            pltpu.VMEM((8, T, 2 * HD), bf16),
            pltpu.VMEM((8, T, 2 * HD), bf16),
            pltpu.VMEM((2, T, 2 * HD), f32),
            pltpu.VMEM((T, 2 * HD), bf16),
            pltpu.VMEM((T, 2 * HD), bf16),
            pltpu.VMEM((32, 16, HD), bf16),
            pltpu.VMEM((32, 16, HD), bf16),
            pltpu.VMEM((16, T, FEAT), bf16),
            pltpu.VMEM((FEAT, 16 * T), bf16),
            pltpu.VMEM((16, T, 2 * HD), bf16),
            pltpu.VMEM((16, 2, 16, 2 * HD), f32),
            pltpu.VMEM((16, 16, 2 * HD), bf16),
            pltpu.VMEM((16, 16, 2 * HD), bf16),
            pltpu.VMEM((16, 16, 2 * HD), bf16),
            pltpu.VMEM((16, 16, 2 * HD), bf16),
            dma((4,)), dma((2,)), dma((2,)), dma((4,)), dma((4,)), dma((8,)), dma((8,)),
            dma((15,)), dma((15,)), dma((8,)), dma((8,)), dma, dma, dma((31,)), dma((31,)),
            dma((15,)), dma((15,)), dma, dma, dma((15,)), dma((15,)),
        ],
        compiler_params=pltpu.CompilerParams(collective_id=0, has_side_effects=True, vmem_limit_bytes=48 * 2**20),
        name="backward",
    )(normed, query, key_value, output_grad, lengths, advantage, span_plan.reshape(32, 32))


def solution(mesh):
    return jax.shard_map(
        local,
        mesh=mesh,
        in_specs=(
            P(("dp", "ctx"), None),
            P(("dp", "ctx"), None),
            P(("dp", "ctx"), None),
            P(("dp", "ctx"), None),
            P("dp", None),
            P("dp", None),
            P("dp", None, None),
        ),
        out_specs=(P(("dp", "ctx"), None), P(("dp", "ctx"), None), P(("ctx", "dp"), None)),
        check_vma=False,
    )
```

time: 889 us -> 120 us (0.13)
  the two profiles are of different devices: /device:TPU:1 before, /device:TPU:7 now
where the time goes in v1:
time: 120 us
  Pallas kernels  111 us (92%)
  local copies, waits for them, and re-layouts  8.14 us (7%)
    pallas_call x1, Pallas kernels, local(): pl.pallas_call(kernel, out_shape=(jax.ShapeDtypeStruct((T, HQ * HD), bf16...  111 us
    unnamed x17, local copies, waits for them, and re-layouts  8.14 us

profile of v1, /device:TPU:7, one launch (start us, length us, event | category | flops | bytes accessed | tf_op | source)
XLA Modules:
  0.0 120.1 jit_solution(14666913987346252386)
XLA Ops:
  0.6 0.0 copy-start
  0.6 1.6 %copy-done = bf16[128,8192]{1,0:T(8,128)(2,1)S(1)} copy-done((bf16[128,8192]{1,0:T(8,128)(2,1)S(1)}, bf16[128,8192]{1,0:T(8,128)(2,1)}, u32[]{:S(2)}) %copy-start) | copy-done | bytes 2097176
  2.2 0.0 copy-start.1
  2.2 0.9 copy-done.1
  3.1 0.0 copy-start.2
  3.1 0.9 copy-done.2
  4.0 0.0 copy-start.3
  4.0 0.8 copy-done.3
  4.9 0.0 copy-start.4
  4.9 0.7 copy-done.4
  5.6 0.0 copy-start.5
  5.6 0.7 copy-done.5
  6.2 0.0 copy-start.6
  6.2 0.7 copy-done.6
  6.9 111.3 %backward.1 = (bf16[128,512]{1,0:T(8,128)(2,1)S(1)}, bf16[128,256]{1,0:T(8,128)(2,1)S(1)}, bf16[16,256]{1,0:T(8,128)(2,1)S(1)}) custom-call(bf16[128,8192]{1,0:T(8,128)(2,1)S(1)} %copy-done, bf16[128,512]{1,0:T(8,128)(2,1)S(1)} %copy-done.1, bf16[128,256]{1,0:T(8,128)(2,1)S(1)} %copy-done.3, bf16[128,512]{1,0:T(8,128)(2,1)S(1)} %copy-done.2, ...), custom_call_target="tpu_custom_call" | custom-call | tf_op jit(solution)/shard_map/backward/pallas_call | solution.py:309
  118.3 0.7 copy.13
  118.9 0.6 copy.14
  119.5 0.6 copy.15
Async XLA Ops:
  0.6 1.6 %copy-start = (bf16[128,8192]{1,0:T(8,128)(2,1)S(1)}, bf16[128,8192]{1,0:T(8,128)(2,1)}, u32[]{:S(2)}) copy-start(bf16[128,8192]{1,0:T(8,128)(2,1)} %normed.1) | copy-start | bytes 6291460
  2.2 0.9 copy-start.1
  3.1 0.9 copy-start.2
  4.0 0.8 copy-start.3
  4.9 0.7 copy-start.4
  5.6 0.7 copy-start.5
  6.2 0.7 copy-start.6

commit v2 on v1

v2 whole, which is shorter than its diff:
```python
import jax
import jax.numpy as jnp
from jax import lax
from jax.experimental import pallas as pl
from jax.experimental.pallas import tpu as pltpu
from jax.sharding import PartitionSpec as P

NEG_FILL = -1e30
MESH = pl.DeviceIdType.MESH
T = 128
HQ = 4
HD = 128
SEEN = 5
FEAT = 512
SCALE = HD**-0.5
OTHERS = [(0, 1), (1, 0), (1, 1), (2, 0), (2, 1), (3, 0), (3, 1)]


def dot_nt(a, b):
    return lax.dot_general(a, b, (((1,), (1,)), ((), ())), preferred_element_type=jnp.float32)


def dot_nn(a, b):
    return lax.dot_general(a, b, (((1,), (0,)), ((), ())), preferred_element_type=jnp.float32)


def kernel(normed, query, kv, og, lengths_in, advantage_in, plan_in, qg_out, kvg_out, wg_out,
           lengths, advantage, plan, q_in, og_in, q_st, o_st, kvb, k_t, bias, p_st, ds_st, onehot, part, got, own_far, far_sum, far_got,
           q_send, q_recv, x_in, x_t, x_all, g_all, w_acc, w_send, w_got, w_z, w_z_got,
           loc_sem, kz_s, kz_r, kp_s, kp_r, kf_s, kf_r, x_s, x_r, d_s, d_r, dz_s, dz_r, qa_s, qa_r, g_s, g_r, w_s, w_r, z_s, z_r):
    d = lax.axis_index("dp")
    c = lax.axis_index("ctx")
    j, p = c // 2, c % 2
    z_lo, core = d // 2, d % 2
    z = p * 8 + z_lo
    y, x = j // 4, lax.rem(j, 4)
    own_slot = (x * 2 + core, y * 2 + core)
    own_pos = (x, y)

    def plane(offset):
        return (d, lax.rem(j + offset, 16) * 2 + p)

    partner = (d, j * 2 + (1 - p))

    def line(axis, offset, flip):
        to_core = core if flip == 0 else 1 - core
        to_x = lax.rem(x + offset, 4) if axis == 0 else x
        to_y = lax.rem(y + offset, 4) if axis == 1 else y
        return (z_lo * 2 + to_core, (to_y * 4 + to_x) * 2 + p)

    def along_z(offset):
        there = lax.rem(z + offset, 16)
        return (lax.rem(there, 8) * 2 + core, j * 2 + there // 8)

    def remote(src, dst, send, recv, where):
        return pltpu.make_async_remote_copy(src_ref=src, dst_ref=dst, send_sem=send, recv_sem=recv,
                                            device_id=where, device_id_type=MESH)

    sends, recvs = [], []

    def launch(*cps):
        for cp in cps:
            cp.start()
            sends.append(cp)
            recvs.append(cp)

    def take(*cps):
        for cp in cps:
            recvs[:] = [r for r in recvs if r is not cp]
            cp.wait_recv()

    def launch_all(make, low, high):
        def step(o, carry):
            make(o).start()
            return carry

        lax.fori_loop(low, high, step, 0)
        sends.append((make, low, high))
        recvs.append((make, low, high))

    def take_all(make, low, high, then=None):
        def step(o, carry):
            make(o).wait_recv()
            if then is not None:
                then(o)
            return carry

        recvs[:] = [r for r in recvs if not (isinstance(r, tuple) and r[0] is make and r[1:] == (low, high))]
        lax.fori_loop(low, high, step, 0)

    loads = [
        pltpu.make_async_copy(query, q_in, loc_sem.at[0]),
        pltpu.make_async_copy(og, og_in, loc_sem.at[1]),
        pltpu.make_async_copy(kv, kvb.at[0], loc_sem.at[2]),
        pltpu.make_async_copy(normed, x_in, loc_sem.at[3]),
        pltpu.make_async_copy(lengths_in, lengths, loc_sem.at[4]),
        pltpu.make_async_copy(advantage_in, advantage, loc_sem.at[5]),
        pltpu.make_async_copy(plan_in.at[0], plan, loc_sem.at[6]),
    ]
    for cp in loads:
        cp.start()

    barrier = pltpu.get_barrier_semaphore()

    def greet_ctx(o, carry):
        pl.semaphore_signal(barrier, inc=1, device_id=(d, lax.rem(c + o, 32)), device_id_type=MESH)
        return carry

    def greet_z(o, carry):
        pl.semaphore_signal(barrier, inc=1, device_id=along_z(o), device_id_type=MESH)
        return carry

    lax.fori_loop(1, 32, greet_ctx, 0)
    lax.fori_loop(1, 8, greet_z, 0)
    lax.fori_loop(9, 16, greet_z, 0)
    for axis, offset in [(0, 0), (0, 1), (0, 2), (0, 3), (1, 1), (1, 2), (1, 3)]:
        pl.semaphore_signal(barrier, inc=1, device_id=line(axis, offset, 1), device_id_type=MESH)
    pl.semaphore_wait(barrier, 52)

    halves = [pl.ds(0, HD), pl.ds(HD, HD)]
    kz = [remote(kv.at[:, half], kvb.at[SEEN, :, half], kz_s.at[i], kz_r.at[i], partner) for i, half in enumerate(halves)]
    launch(*kz)
    kp = [remote(kv, kvb.at[o], kp_s.at[o - 1], kp_r.at[o - 1], plane(o)) for o in range(1, SEEN)]
    launch(*kp)

    loads[3].wait()

    def turn(at, carry):
        for q in range(4):
            block = x_in[:, pl.ds(pl.multiple_of(at * FEAT + q * T, T), T)].T
            for low in range(4):
                for k in range(2):
                    x_t[q // 2, k, at // 4, lax.rem(at, 4), pl.ds(((q % 2) * 4 + low) * 16, 16), :] = (
                        block[(low * 2 + k) * 16 : (low * 2 + k + 1) * 16])
        return carry

    lax.fori_loop(0, 16, turn, 0)

    def x_source(axis, offset, flip):
        to_core = core if flip == 0 else 1 - core
        if axis == 0:
            return x_t.at[0, to_core, :, lax.rem(x + offset, 4)]
        return x_t.at[1, to_core, lax.rem(y + offset, 4)]

    def x_place(axis):
        return x_all.at[axis, :, :, pl.ds(pl.multiple_of(own_slot[axis] * T, T), T)]

    x_copies = {}
    for axis in range(2):
        for offset, flip in OTHERS:
            m = axis * 7 + offset * 2 + flip - 1
            x_copies[axis, offset, flip] = remote(x_source(axis, offset, flip), x_place(axis), x_s.at[m], x_r.at[m], line(axis, offset, flip))
    x_own = [pltpu.make_async_copy(x_source(axis, 0, 0), x_place(axis), loc_sem.at[7 + axis]) for axis in range(2)]
    for cp in x_own:
        cp.start()
    launch(*[cp for (axis, offset, flip), cp in x_copies.items() if offset != 2])

    for cp in loads[4:]:
        cp.wait()
    lanes = lax.broadcasted_iota(jnp.int32, (1, T), 1)
    rows = lax.broadcasted_iota(jnp.int32, (T, HD), 0)
    pos_lane = c * T + lanes
    pos_row = c * T + rows
    start_lane = jnp.zeros((1, T), jnp.int32)
    adv_row = jnp.zeros((T, HD), jnp.float32)
    end = jnp.int32(0)
    for i in range(16):
        begin = end
        end = end + lengths[0, i]
        start_lane = jnp.where(pos_lane >= begin, begin, start_lane)
        adv_row = jnp.where(pos_row >= begin, advantage[0, i], adv_row)
    key_rows = lax.broadcasted_iota(jnp.int32, (T, T), 0)
    for rel in range(2):
        for o in range(SEEN):
            key_plane = p if rel == 0 else 1 - p
            base = ((j - o) * 2 + key_plane) * T
            seen = (key_rows >= start_lane - base) & (key_rows <= pos_lane - base)
            bias[pl.ds((rel * SEEN + o) * T, T), :] = jnp.where(seen, 0.0, NEG_FILL)

    plan_row = plan[pl.ds(c, 1), :]
    out_row = lax.broadcasted_iota(jnp.int32, (4 * T, 32), 0)
    span_no = lax.broadcasted_iota(jnp.int32, (4 * T, 32), 1)
    block = jnp.sum(jnp.where(out_row // 16 == span_no, jnp.broadcast_to(plan_row, (4 * T, 32)), 0), axis=1, keepdims=True)
    row_no = lax.broadcasted_iota(jnp.int32, (4 * T, 1), 0)
    source = (row_no // 4 % 4) * T + block * 4 + row_no % 4
    for h in range(HQ):
        col_no = lax.broadcasted_iota(jnp.int32, (4 * T, T), 1) + h * T
        onehot[:, pl.ds(h * T, T)] = jnp.where(col_no == source, 1.0, 0.0).astype(jnp.bfloat16)

    loads[0].wait()
    loads[1].wait()
    for h in range(HQ):
        cols = pl.ds(h * HD, HD)
        q_st[pl.ds(h * T, T), :] = q_in[:, cols]
        o_st[pl.ds(h * T, T), :] = (adv_row * og_in[:, cols].astype(jnp.float32)).astype(jnp.bfloat16)

    kf = []
    for i, half in enumerate(halves):
        take(kz[i])
        for o in range(1, SEEN):
            cp = remote(kvb.at[SEEN, :, half], kvb.at[SEEN + o, :, half], kf_s.at[i * 4 + o - 1], kf_r.at[i * 4 + o - 1], plane(o))
            launch(cp)
            kf.append(cp)
    loads[2].wait()
    take(*kp)
    take(*kf)

    n_keys = 2 * SEEN * T
    keys = kvb[:, :, :HD].reshape(n_keys, HD)
    values = kvb[:, :, HD:].reshape(n_keys, HD)
    for s in range(2 * SEEN):
        k_t[:, pl.ds(s * T, T)] = kvb[s, :, :HD].T
    for h in range(HQ):
        heads = pl.ds(h * T, T)
        scores = dot_nt(keys, q_st[heads, :]) * SCALE + bias[...]
        top = jnp.max(scores, axis=0, keepdims=True)
        weights = jnp.exp(scores - top)
        probs = weights * (1.0 / jnp.sum(weights, axis=0, keepdims=True))
        grad_prob = dot_nt(values, o_st[heads, :])
        row_dot = jnp.sum(probs * grad_prob, axis=0, keepdims=True)
        ds_st[:, heads] = (probs * (grad_prob - row_dot)).astype(jnp.bfloat16)
        p_st[:, heads] = probs.astype(jnp.bfloat16)

    half_rows = SEEN * T

    def grads(rel):
        at = pl.ds(rel * half_rows, half_rows)
        dk = dot_nn(ds_st[at, :], q_st[...]) * SCALE
        dv = dot_nn(p_st[at, :], o_st[...])
        return jnp.concatenate([dk, dv], axis=1)

    sent = []
    for rel in (1, 0):
        terms = grads(rel)
        own_far[rel] = terms[:T]
        part[pl.ds(rel * 4, 4)] = terms[T:].astype(jnp.bfloat16).reshape(SEEN - 1, T, 2 * HD)
        for o in range(1, SEEN):
            i = rel * 4 + o - 1
            cp = remote(part.at[i], got.at[i], d_s.at[i], d_r.at[i], plane(16 - o))
            launch(cp)
            sent.append((rel, cp))

    q_grad_t = (dot_nn(k_t[...], ds_st[...]) * SCALE).astype(jnp.bfloat16)
    q_send[...] = dot_nt(onehot[...], q_grad_t).astype(jnp.bfloat16).reshape(32, 16, HD)
    q_recv[c] = q_send[c]

    def terms_sum(rel):
        for r, cp in sent:
            if r == rel:
                take(cp)
        total = own_far[rel]
        for o in range(SEEN - 1):
            total = total + got[rel * 4 + o].astype(jnp.float32)
        return total

    far_sum[...] = terms_sum(1).astype(jnp.bfloat16)
    dz = remote(far_sum, far_got, dz_s, dz_r, partner)
    launch(dz)

    launch(*[cp for (axis, offset, flip), cp in x_copies.items() if offset == 2])

    near = terms_sum(0)

    take(dz)
    kvg = (near + far_got[...].astype(jnp.float32)).astype(jnp.bfloat16)
    g_copies = []
    for axis in range(2):
        g_all[axis, own_slot[axis]] = kvg
        for offset, flip in OTHERS:
            m = axis * 7 + offset * 2 + flip - 1
            slot = g_all.at[axis, own_slot[axis]]
            g_copies.append((axis, remote(slot, slot, g_s.at[m], g_r.at[m], line(axis, offset, flip))))
    launch(*[cp for _, cp in g_copies])
    kvg_out[...] = kvg

    def q_copy(o):
        there = lax.rem(c + o, 32)
        return remote(q_send.at[there], q_recv.at[c], qa_s.at[o - 1], qa_r.at[o - 1], (d, there))

    launch_all(q_copy, 1, 32)

    take(*x_copies.values())
    for cp in x_own:
        cp.wait()

    w_copies = []
    for axis in range(2):
        take(*[cp for a, cp in g_copies if a == axis])
        w_acc[axis] = dot_nn(x_all[axis].reshape(4 * T, 8 * T), g_all[axis].reshape(8 * T, 2 * HD)).reshape(4, T, 2 * HD)
        w_send[axis] = w_acc[axis].astype(jnp.bfloat16)
        for offset in range(1, 4):
            m = axis * 3 + offset - 1
            there = lax.rem(own_pos[1 - axis] + offset, 4)
            cp = remote(w_send.at[axis, there], w_got.at[m], w_s.at[m], w_r.at[m], line(1 - axis, offset, 0))
            launch(cp)
            w_copies.append((axis, cp))
    for axis in range(2):
        take(*[cp for a, cp in w_copies if a == axis])
        total = w_acc[axis, own_pos[1 - axis]]
        for offset in range(1, 4):
            total = total + w_got[axis * 3 + offset - 1].astype(jnp.float32)
        w_z[pl.ds(axis * 8, 8)] = total.astype(jnp.bfloat16).reshape(8, 16, 2 * HD)
    w_z_got[z] = w_z[z]

    def z_copy(o):
        return remote(w_z.at[lax.rem(z + o, 16)], w_z_got.at[z], z_s.at[o - 1], z_r.at[o - 1], along_z(o))

    launch_all(z_copy, 1, 16)

    take_all(q_copy, 1, 32)
    arrived = q_recv[...].reshape(4 * T, HD)
    tok = lax.broadcasted_iota(jnp.int32, (T, 4 * T), 0)
    place = lax.broadcasted_iota(jnp.int32, (T, 4 * T), 1)
    for h in range(HQ):
        pick = jnp.where(place == tok // 4 * 16 + h * 4 + tok % 4, 1.0, 0.0).astype(jnp.bfloat16)
        qg_out[:, pl.ds(h * HD, HD)] = dot_nn(pick, arrived).astype(jnp.bfloat16)

    take_all(z_copy, 1, 16)
    total = jnp.sum(w_z_got[...].astype(jnp.float32), axis=0)
    wg_out[...] = (total * (1.0 / 256.0)).astype(jnp.bfloat16)

    for item in sends:
        if isinstance(item, tuple):
            make, low, high = item

            def step(o, carry, make=make):
                make(o).wait_send()
                return carry

            lax.fori_loop(low, high, step, 0)
        else:
            item.wait_send()

def local(normed, query, key_value, output_grad, lengths, advantage, span_plan):
    bf16, f32 = jnp.bfloat16, jnp.float32
    n_keys = 2 * SEEN * T
    dma = pltpu.SemaphoreType.DMA
    vmem = pl.BlockSpec(memory_space=pltpu.VMEM)
    return pl.pallas_call(
        kernel,
        out_shape=(
            jax.ShapeDtypeStruct((T, HQ * HD), bf16),
            jax.ShapeDtypeStruct((T, 2 * HD), bf16),
            jax.ShapeDtypeStruct((16, 2 * HD), bf16),
        ),
        in_specs=[pl.BlockSpec(memory_space=pltpu.HBM)] * 7,
        out_specs=(vmem, vmem, vmem),
        scratch_shapes=[
            pltpu.SMEM((1, 16), jnp.int32),
            pltpu.SMEM((1, 16), f32),
            pltpu.VMEM((32, 32), jnp.int32),
            pltpu.VMEM((T, HQ * HD), bf16),
            pltpu.VMEM((T, HQ * HD), bf16),
            pltpu.VMEM((HQ * T, HD), bf16),
            pltpu.VMEM((HQ * T, HD), bf16),
            pltpu.VMEM((2 * SEEN, T, 2 * HD), bf16),
            pltpu.VMEM((HD, n_keys), bf16),
            pltpu.VMEM((n_keys, T), f32),
            pltpu.VMEM((n_keys, HQ * T), bf16),
            pltpu.VMEM((n_keys, HQ * T), bf16),
            pltpu.VMEM((HQ * T, HQ * T), bf16),
            pltpu.VMEM((8, T, 2 * HD), bf16),
            pltpu.VMEM((8, T, 2 * HD), bf16),
            pltpu.VMEM((2, T, 2 * HD), f32),
            pltpu.VMEM((T, 2 * HD), bf16),
            pltpu.VMEM((T, 2 * HD), bf16),
            pltpu.VMEM((32, 16, HD), bf16),
            pltpu.VMEM((32, 16, HD), bf16),
            pltpu.VMEM((T, 16 * FEAT), bf16),
            pltpu.VMEM((2, 2, 4, 4, T, T), bf16),
            pltpu.VMEM((2, 4, T, 8 * T), bf16),
            pltpu.VMEM((2, 8, T, 2 * HD), bf16),
            pltpu.VMEM((2, 4, T, 2 * HD), f32),
            pltpu.VMEM((2, 4, T, 2 * HD), bf16),
            pltpu.VMEM((6, T, 2 * HD), bf16),
            pltpu.VMEM((16, 16, 2 * HD), bf16),
            pltpu.VMEM((16, 16, 2 * HD), bf16),
            dma((9,)), dma((2,)), dma((2,)), dma((4,)), dma((4,)), dma((8,)), dma((8,)),
            dma((14,)), dma((14,)), dma((8,)), dma((8,)), dma, dma, dma((31,)), dma((31,)),
            dma((14,)), dma((14,)), dma((6,)), dma((6,)), dma((15,)), dma((15,)),
        ],
        compiler_params=pltpu.CompilerParams(collective_id=0, has_side_effects=True, vmem_limit_bytes=54 * 2**20),
        name="backward",
    )(normed, query, key_value, output_grad, lengths, advantage, span_plan)


def solution(mesh):
    return jax.shard_map(
        local,
        mesh=mesh,
        in_specs=(
            P(("dp", "ctx"), None),
            P(("dp", "ctx"), None),
            P(("dp", "ctx"), None),
            P(("dp", "ctx"), None),
            P("dp", None),
            P("dp", None),
            P("dp", None, None),
        ),
        out_specs=(P(("dp", "ctx"), None), P(("dp", "ctx"), None), P(("ctx", "dp"), None)),
        check_vma=False,
    )
```

time: 120 us -> 93.4 us (0.78)
  the two profiles are of different devices: /device:TPU:7 before, /device:TPU:1 now
where the time goes in v2:
time: 93.4 us; the launch traced here: 93.2 us
  Pallas kernels  88.2 us (94%)
  local copies, waits for them, and re-layouts  4.34 us (5%)
    pallas_call x1, Pallas kernels, local(): pl.pallas_call(kernel, out_shape=(jax.ShapeDtypeStruct((T, HQ * HD), bf16...  88.2 us
    unnamed x3, local copies, waits for them, and re-layouts  4.34 us

profile of v2, /device:TPU:1, one launch (start us, length us, event | category | flops | bytes accessed | tf_op | source)
XLA Modules:
  0.0 93.2 jit_solution(13344495739763172293)
XLA Ops:
  0.6 88.2 %backward.1 = (bf16[128,512]{1,0:T(8,128)(2,1)}, bf16[128,256]{1,0:T(8,128)(2,1)}, bf16[16,256]{1,0:T(8,128)(2,1)}) custom-call(bf16[128,8192]{1,0:T(8,128)(2,1)} %normed.1, bf16[128,512]{1,0:T(8,128)(2,1)} %query.1, bf16[128,256]{1,0:T(8,128)(2,1)} %kv.1, bf16[128,512]{1,0:T(8,128)(2,1)} %og.1, s32[1,16]{1,0:T(1,128)} %lengths_in.1, f32[1,16]{1,0:T(1,128)} %advantage_in.1, ...), custom_call_target="tpu_custom_call" | custom-call | tf_op jit(solution)/shard_map/backward/pallas_call | solution.py:339
  88.8 1.6 %copy.13 = bf16[128,512]{1,0:T(8,128)(2,1)} copy(bf16[128,512]{1,0:T(8,128)(2,1)} %get-tuple-element.6) | data formatting | bytes 262144
  90.4 1.5 %copy.14 = bf16[128,256]{1,0:T(8,128)(2,1)} copy(bf16[128,256]{1,0:T(8,128)(2,1)} %get-tuple-element.7) | data formatting | bytes 131072
  91.9 1.3 %copy.15 = bf16[16,256]{1,0:T(8,128)(2,1)} copy(bf16[16,256]{1,0:T(8,128)(2,1)} %get-tuple-element.8) | data formatting | bytes 16384

commit v3 on v2

--- a/solution.py
+++ b/solution.py
@@ -13,7 +13,9 @@
 SEEN = 5
 FEAT = 512
 SCALE = HD**-0.5
-OTHERS = [(0, 1), (1, 0), (1, 1), (2, 0), (2, 1), (3, 0), (3, 1)]
+OTHERS = [(2, 0), (2, 1), (1, 0), (1, 1), (3, 0), (3, 1), (0, 1)]
+VALUE, KEY = 0, 1
+COLUMNS = [pl.ds(HD, HD), pl.ds(0, HD)]
 
 
 def dot_nt(a, b):
@@ -88,6 +90,21 @@
         recvs[:] = [r for r in recvs if not (isinstance(r, tuple) and r[0] is make and r[1:] == (low, high))]
         lax.fori_loop(low, high, step, 0)
 
+    barrier = pltpu.get_barrier_semaphore()
+
+    def greet_ctx(o, carry):
+        pl.semaphore_signal(barrier, inc=1, device_id=(d, lax.rem(c + o, 32)), device_id_type=MESH)
+        return carry
+
+    def greet_z(o, carry):
+        pl.semaphore_signal(barrier, inc=1, device_id=along_z(o), device_id_type=MESH)
+        return carry
+
+    lax.fori_loop(1, 32, greet_ctx, 0)
+    lax.fori_loop(1, 8, greet_z, 0)
+    lax.fori_loop(9, 16, greet_z, 0)
+    for axis, offset in [(0, 0), (0, 1), (0, 2), (0, 3), (1, 1), (1, 2), (1, 3)]:
+        pl.semaphore_signal(barrier, inc=1, device_id=line(axis, offset, 1), device_id_type=MESH)
     loads = [
         pltpu.make_async_copy(query, q_in, loc_sem.at[0]),
         pltpu.make_async_copy(og, og_in, loc_sem.at[1]),
@@ -100,21 +117,6 @@
     for cp in loads:
         cp.start()
 
-    barrier = pltpu.get_barrier_semaphore()
-
-    def greet_ctx(o, carry):
-        pl.semaphore_signal(barrier, inc=1, device_id=(d, lax.rem(c + o, 32)), device_id_type=MESH)
-        return carry
-
-    def greet_z(o, carry):
-        pl.semaphore_signal(barrier, inc=1, device_id=along_z(o), device_id_type=MESH)
-        return carry
-
-    lax.fori_loop(1, 32, greet_ctx, 0)
-    lax.fori_loop(1, 8, greet_z, 0)
-    lax.fori_loop(9, 16, greet_z, 0)
-    for axis, offset in [(0, 0), (0, 1), (0, 2), (0, 3), (1, 1), (1, 2), (1, 3)]:
-        pl.semaphore_signal(barrier, inc=1, device_id=line(axis, offset, 1), device_id_type=MESH)
     pl.semaphore_wait(barrier, 52)
 
     halves = [pl.ds(0, HD), pl.ds(HD, HD)]
@@ -177,6 +179,20 @@
             seen = (key_rows >= start_lane - base) & (key_rows <= pos_lane - base)
             bias[pl.ds((rel * SEEN + o) * T, T), :] = jnp.where(seen, 0.0, NEG_FILL)
 
+    loads[0].wait()
+    loads[1].wait()
+    for h in range(HQ):
+        cols = pl.ds(h * HD, HD)
+        q_st[pl.ds(h * T, T), :] = q_in[:, cols]
+        o_st[pl.ds(h * T, T), :] = (adv_row * og_in[:, cols].astype(jnp.float32)).astype(jnp.bfloat16)
+
+    kf = []
+    for i, half in enumerate(halves):
+        take(kz[i])
+        for o in range(1, SEEN):
+            cp = remote(kvb.at[SEEN, :, half], kvb.at[SEEN + o, :, half], kf_s.at[i * 4 + o - 1], kf_r.at[i * 4 + o - 1], plane(o))
+            launch(cp)
+            kf.append(cp)
     plan_row = plan[pl.ds(c, 1), :]
     out_row = lax.broadcasted_iota(jnp.int32, (4 * T, 32), 0)
     span_no = lax.broadcasted_iota(jnp.int32, (4 * T, 32), 1)
@@ -187,20 +203,6 @@
         col_no = lax.broadcasted_iota(jnp.int32, (4 * T, T), 1) + h * T
         onehot[:, pl.ds(h * T, T)] = jnp.where(col_no == source, 1.0, 0.0).astype(jnp.bfloat16)
 
-    loads[0].wait()
-    loads[1].wait()
-    for h in range(HQ):
-        cols = pl.ds(h * HD, HD)
-        q_st[pl.ds(h * T, T), :] = q_in[:, cols]
-        o_st[pl.ds(h * T, T), :] = (adv_row * og_in[:, cols].astype(jnp.float32)).astype(jnp.bfloat16)
-
-    kf = []
-    for i, half in enumerate(halves):
-        take(kz[i])
-        for o in range(1, SEEN):
-            cp = remote(kvb.at[SEEN, :, half], kvb.at[SEEN + o, :, half], kf_s.at[i * 4 + o - 1], kf_r.at[i * 4 + o - 1], plane(o))
-            launch(cp)
-            kf.append(cp)
     loads[2].wait()
     take(*kp)
     take(*kf)
@@ -223,89 +225,100 @@
 
     half_rows = SEEN * T
 
-    def grads(rel):
+    def term(rel, half):
         at = pl.ds(rel * half_rows, half_rows)
-        dk = dot_nn(ds_st[at, :], q_st[...]) * SCALE
-        dv = dot_nn(p_st[at, :], o_st[...])
-        return jnp.concatenate([dk, dv], axis=1)
-
-    sent = []
+        if half == VALUE:
+            return dot_nn(p_st[at, :], o_st[...])
+        return dot_nn(ds_st[at, :], q_st[...]) * SCALE
+
+    sent = {}
     for rel in (1, 0):
-        terms = grads(rel)
-        own_far[rel] = terms[:T]
-        part[pl.ds(rel * 4, 4)] = terms[T:].astype(jnp.bfloat16).reshape(SEEN - 1, T, 2 * HD)
-        for o in range(1, SEEN):
-            i = rel * 4 + o - 1
-            cp = remote(part.at[i], got.at[i], d_s.at[i], d_r.at[i], plane(16 - o))
-            launch(cp)
-            sent.append((rel, cp))
+        for half in (VALUE, KEY):
+            terms = term(rel, half)
+            own_far[half, rel] = terms[:T]
+            part[half, pl.ds(rel * 4, 4)] = terms[T:].astype(jnp.bfloat16).reshape(SEEN - 1, T, HD)
+            sent[rel, half] = []
+            for o in range(1, SEEN):
+                i = rel * 4 + o - 1
+                cp = remote(part.at[half, i], got.at[half, i], d_s.at[half, i], d_r.at[half, i], plane(16 - o))
+                launch(cp)
+                sent[rel, half].append(cp)
 
     q_grad_t = (dot_nn(k_t[...], ds_st[...]) * SCALE).astype(jnp.bfloat16)
     q_send[...] = dot_nt(onehot[...], q_grad_t).astype(jnp.bfloat16).reshape(32, 16, HD)
     q_recv[c] = q_send[c]
 
-    def terms_sum(rel):
-        for r, cp in sent:
-            if r == rel:
-                take(cp)
-        total = own_far[rel]
+    def terms_sum(rel, half):
+        take(*sent[rel, half])
+        total = own_far[half, rel]
         for o in range(SEEN - 1):
-            total = total + got[rel * 4 + o].astype(jnp.float32)
+            total = total + got[half, rel * 4 + o].astype(jnp.float32)
         return total
 
-    far_sum[...] = terms_sum(1).astype(jnp.bfloat16)
-    dz = remote(far_sum, far_got, dz_s, dz_r, partner)
-    launch(dz)
-
+    dz = []
+    for half in (VALUE, KEY):
+        far_sum[half] = terms_sum(1, half).astype(jnp.bfloat16)
+        dz.append(remote(far_sum.at[half], far_got.at[half], dz_s.at[half], dz_r.at[half], partner))
+        launch(dz[half])
     launch(*[cp for (axis, offset, flip), cp in x_copies.items() if offset == 2])
-
-    near = terms_sum(0)
-
-    take(dz)
-    kvg = (near + far_got[...].astype(jnp.float32)).astype(jnp.bfloat16)
-    g_copies = []
-    for axis in range(2):
-        g_all[axis, own_slot[axis]] = kvg
-        for offset, flip in OTHERS:
-            m = axis * 7 + offset * 2 + flip - 1
-            slot = g_all.at[axis, own_slot[axis]]
-            g_copies.append((axis, remote(slot, slot, g_s.at[m], g_r.at[m], line(axis, offset, flip))))
-    launch(*[cp for _, cp in g_copies])
-    kvg_out[...] = kvg
-
     def q_copy(o):
         there = lax.rem(c + o, 32)
         return remote(q_send.at[there], q_recv.at[c], qa_s.at[o - 1], qa_r.at[o - 1], (d, there))
 
     launch_all(q_copy, 1, 32)
 
+    near = [terms_sum(0, half) for half in (VALUE, KEY)]
+
+    g_copies = {}
+    for half in (VALUE, KEY):
+        take(dz[half])
+        kvg = (near[half] + far_got[half].astype(jnp.float32)).astype(jnp.bfloat16)
+        kvg_out[:, COLUMNS[half]] = kvg
+        for axis in range(2):
+            g_all[half, axis, own_slot[axis]] = kvg
+        for axis in range(2):
+            g_copies[half, axis] = []
+            for offset, flip in OTHERS:
+                m = axis * 7 + offset * 2 + flip - 1
+                slot = g_all.at[half, axis, own_slot[axis]]
+                cp = remote(slot, slot, g_s.at[half, m], g_r.at[half, m], line(axis, offset, flip))
+                launch(cp)
+                g_copies[half, axis].append(cp)
+
     take(*x_copies.values())
     for cp in x_own:
         cp.wait()
 
-    w_copies = []
-    for axis in range(2):
-        take(*[cp for a, cp in g_copies if a == axis])
-        w_acc[axis] = dot_nn(x_all[axis].reshape(4 * T, 8 * T), g_all[axis].reshape(8 * T, 2 * HD)).reshape(4, T, 2 * HD)
-        w_send[axis] = w_acc[axis].astype(jnp.bfloat16)
-        for offset in range(1, 4):
-            m = axis * 3 + offset - 1
-            there = lax.rem(own_pos[1 - axis] + offset, 4)
-            cp = remote(w_send.at[axis, there], w_got.at[m], w_s.at[m], w_r.at[m], line(1 - axis, offset, 0))
-            launch(cp)
-            w_copies.append((axis, cp))
-    for axis in range(2):
-        take(*[cp for a, cp in w_copies if a == axis])
-        total = w_acc[axis, own_pos[1 - axis]]
-        for offset in range(1, 4):
-            total = total + w_got[axis * 3 + offset - 1].astype(jnp.float32)
-        w_z[pl.ds(axis * 8, 8)] = total.astype(jnp.bfloat16).reshape(8, 16, 2 * HD)
-    w_z_got[z] = w_z[z]
-
-    def z_copy(o):
-        return remote(w_z.at[lax.rem(z + o, 16)], w_z_got.at[z], z_s.at[o - 1], z_r.at[o - 1], along_z(o))
-
-    launch_all(z_copy, 1, 16)
+    w_copies = {}
+    for half in (VALUE, KEY):
+        for axis in range(2):
+            take(*g_copies[half, axis])
+            terms = dot_nn(x_all[axis].reshape(4 * T, 8 * T), g_all[half, axis].reshape(8 * T, HD)).reshape(4, T, HD)
+            w_acc[half, axis] = terms
+            w_send[half, axis] = terms.astype(jnp.bfloat16)
+            w_copies[half, axis] = []
+            for offset in (2, 1, 3):
+                m = axis * 3 + offset - 1
+                there = lax.rem(own_pos[1 - axis] + offset, 4)
+                cp = remote(w_send.at[half, axis, there], w_got.at[half, m], w_s.at[half, m], w_r.at[half, m], line(1 - axis, offset, 0))
+                launch(cp)
+                w_copies[half, axis].append(cp)
+
+    z_copies = []
+    for half in (VALUE, KEY):
+        for axis in range(2):
+            take(*w_copies[half, axis])
+            total = w_acc[half, axis, own_pos[1 - axis]]
+            for offset in range(1, 4):
+                total = total + w_got[half, axis * 3 + offset - 1].astype(jnp.float32)
+            w_z[half, pl.ds(axis * 8, 8)] = total.astype(jnp.bfloat16).reshape(8, 16, HD)
+        w_z_got[half, z] = w_z[half, z]
+
+        def z_copy(o, half=half):
+            return remote(w_z.at[half, lax.rem(z + o, 16)], w_z_got.at[half, z], z_s.at[half, o - 1], z_r.at[half, o - 1], along_z(o))
+
+        launch_all(z_copy, 1, 16)
+        z_copies.append(z_copy)
 
     take_all(q_copy, 1, 32)
     arrived = q_recv[...].reshape(4 * T, HD)
@@ -315,9 +328,10 @@
         pick = jnp.where(place == tok // 4 * 16 + h * 4 + tok % 4, 1.0, 0.0).astype(jnp.bfloat16)
         qg_out[:, pl.ds(h * HD, HD)] = dot_nn(pick, arrived).astype(jnp.bfloat16)
 
-    take_all(z_copy, 1, 16)
-    total = jnp.sum(w_z_got[...].astype(jnp.float32), axis=0)
-    wg_out[...] = (total * (1.0 / 256.0)).astype(jnp.bfloat16)
+    for half in (VALUE, KEY):
+        take_all(z_copies[half], 1, 16)
+        total = jnp.sum(w_z_got[half].astype(jnp.float32), axis=0)
+        wg_out[:, COLUMNS[half]] = (total * (1.0 / 256.0)).astype(jnp.bfloat16)
 
     for item in sends:
         if isinstance(item, tuple):
@@ -359,29 +373,29 @@
             pltpu.VMEM((n_keys, HQ * T), bf16),
             pltpu.VMEM((n_keys, HQ * T), bf16),
             pltpu.VMEM((HQ * T, HQ * T), bf16),
-            pltpu.VMEM((8, T, 2 * HD), bf16),
-            pltpu.VMEM((8, T, 2 * HD), bf16),
-            pltpu.VMEM((2, T, 2 * HD), f32),
-            pltpu.VMEM((T, 2 * HD), bf16),
-            pltpu.VMEM((T, 2 * HD), bf16),
+            pltpu.VMEM((2, 8, T, HD), bf16),
+            pltpu.VMEM((2, 8, T, HD), bf16),
+            pltpu.VMEM((2, 2, T, HD), f32),
+            pltpu.VMEM((2, T, HD), bf16),
+            pltpu.VMEM((2, T, HD), bf16),
             pltpu.VMEM((32, 16, HD), bf16),
             pltpu.VMEM((32, 16, HD), bf16),
             pltpu.VMEM((T, 16 * FEAT), bf16),
             pltpu.VMEM((2, 2, 4, 4, T, T), bf16),
             pltpu.VMEM((2, 4, T, 8 * T), bf16),
-            pltpu.VMEM((2, 8, T, 2 * HD), bf16),
-            pltpu.VMEM((2, 4, T, 2 * HD), f32),
-            pltpu.VMEM((2, 4, T, 2 * HD), bf16),
-            pltpu.VMEM((6, T, 2 * HD), bf16),
-            pltpu.VMEM((16, 16, 2 * HD), bf16),
-            pltpu.VMEM((16, 16, 2 * HD), bf16),
+            pltpu.VMEM((2, 2, 8, T, HD), bf16),
+            pltpu.VMEM((2, 2, 4, T, HD), f32),
+            pltpu.VMEM((2, 2, 4, T, HD), bf16),
+            pltpu.VMEM((2, 6, T, HD), bf16),
+            pltpu.VMEM((2, 16, 16, HD), bf16),
+            pltpu.VMEM((2, 16, 16, HD), bf16),
             dma((9,)), dma((2,)), dma((2,)), dma((4,)), dma((4,)), dma((8,)), dma((8,)),
-            dma((14,)), dma((14,)), dma((8,)), dma((8,)), dma, dma, dma((31,)), dma((31,)),
-            dma((14,)), dma((14,)), dma((6,)), dma((6,)), dma((15,)), dma((15,)),
+            dma((14,)), dma((14,)), dma((2, 8)), dma((2, 8)), dma((2,)), dma((2,)), dma((31,)), dma((31,)),
+            dma((2, 14)), dma((2, 14)), dma((2, 6)), dma((2, 6)), dma((2, 15)), dma((2, 15)),
         ],
-        compiler_params=pltpu.CompilerParams(collective_id=0, has_side_effects=True, vmem_limit_bytes=54 * 2**20),
+        compiler_params=pltpu.CompilerParams(collective_id=0, has_side_effects=True, vmem_limit_bytes=48 * 2**20),
         name="backward",
-    )(normed, query, key_value, output_grad, lengths, advantage, span_plan)
+    )(*[pltpu.with_memory_space_constraint(a, pltpu.HBM) for a in (normed, query, key_value, output_grad, lengths, advantage, span_plan)])
 
 
 def solution(mesh):

time: 93.4 us -> 83.7 us (0.90)
  Pallas kernels: 88.2 us -> 81 us
  local copies, waits for them, and re-layouts: 4.34 us -> 1.88 us
    pallas_call x1, Pallas kernels: 88.2 us -> 81 us  [local(): pl.pallas_call(kernel, out_shape=(jax.ShapeDtypeStruct((T, HQ * HD), bf16...]
    unnamed x3, local copies, waits for them, and re-layouts: 4.34 us -> 1.88 us
where the time goes in v3:
time: 83.7 us; the launch traced here: 83.6 us
  Pallas kernels  81 us (97%)
  local copies, waits for them, and re-layouts  1.88 us (2%)
    pallas_call x1, Pallas kernels, local(): pl.pallas_call(kernel, out_shape=(jax.ShapeDtypeStruct((T, HQ * HD), bf16...  81 us
    unnamed x3, local copies, waits for them, and re-layouts  1.88 us

profile of v3, /device:TPU:1, one launch (start us, length us, event | category | flops | bytes accessed | tf_op | source)
XLA Modules:
  0.0 83.6 jit_solution(778715627489947907)
XLA Ops:
  0.6 81.0 %backward.1 = (bf16[128,512]{1,0:T(8,128)(2,1)S(1)}, bf16[128,256]{1,0:T(8,128)(2,1)S(1)}, bf16[16,256]{1,0:T(8,128)(2,1)S(1)}) custom-call(bf16[128,8192]{1,0:T(8,128)(2,1)} %normed.1, bf16[128,512]{1,0:T(8,128)(2,1)} %query.1, bf16[128,256]{1,0:T(8,128)(2,1)} %kv.1, bf16[128,512]{1,0:T(8,128)(2,1)} %og.1, s32[1,16]{1,0:T(1,128)} %lengths_in.1, ...), custom_call_target="tpu_custom_call" | custom-call | tf_op jit(solution)/shard_map/backward/pallas_call | solution.py:353
  81.7 0.7 copy.13
  82.3 0.6 copy.14
  83.0 0.6 copy.15

commit v4 on v3

--- a/solution.py
+++ b/solution.py
@@ -27,7 +27,7 @@
 
 
 def kernel(normed, query, kv, og, lengths_in, advantage_in, plan_in, qg_out, kvg_out, wg_out,
-           lengths, advantage, plan, q_in, og_in, q_st, o_st, kvb, k_t, bias, p_st, ds_st, onehot, part, got, own_far, far_sum, far_got,
+           lengths, advantage, plan, q_in, og_in, q_st, o_st, kvb, k_t, bias, score, grad_prob, p_st, ds_st, onehot, part, got, own_far, far_sum, far_got,
            q_send, q_recv, x_in, x_t, x_all, g_all, w_acc, w_send, w_got, w_z, w_z_got,
            loc_sem, kz_s, kz_r, kp_s, kp_r, kf_s, kf_r, x_s, x_r, d_s, d_r, dz_s, dz_r, qa_s, qa_r, g_s, g_r, w_s, w_r, z_s, z_r):
     d = lax.axis_index("dp")
@@ -58,51 +58,46 @@
         return pltpu.make_async_remote_copy(src_ref=src, dst_ref=dst, send_sem=send, recv_sem=recv,
                                             device_id=where, device_id_type=MESH)
 
-    sends, recvs = [], []
-
-    def launch(*cps):
+    sends = []
+
+    def whole(ref, send, recv):
+        return remote(ref, ref, send, recv, partner)
+
+    def start(cps, group):
         for cp in cps:
             cp.start()
-            sends.append(cp)
-            recvs.append(cp)
-
-    def take(*cps):
-        for cp in cps:
-            recvs[:] = [r for r in recvs if r is not cp]
-            cp.wait_recv()
-
-    def launch_all(make, low, high):
+        sends.append(group)
+
+    def start_all(make, low, high):
         def step(o, carry):
             make(o).start()
             return carry
 
         lax.fori_loop(low, high, step, 0)
-        sends.append((make, low, high))
-        recvs.append((make, low, high))
-
-    def take_all(make, low, high, then=None):
-        def step(o, carry):
-            make(o).wait_recv()
-            if then is not None:
-                then(o)
-            return carry
-
-        recvs[:] = [r for r in recvs if not (isinstance(r, tuple) and r[0] is make and r[1:] == (low, high))]
-        lax.fori_loop(low, high, step, 0)
+
+    def drain(items):
+        for cp in items:
+            cp.wait_send()
 
     barrier = pltpu.get_barrier_semaphore()
 
-    def greet_ctx(o, carry):
-        pl.semaphore_signal(barrier, inc=1, device_id=(d, lax.rem(c + o, 32)), device_id_type=MESH)
+    def greet_far(o, carry):
+        there = lax.rem(j + o, 16) * 2 + (1 - p)
+        pl.semaphore_signal(barrier, inc=1, device_id=(d, there), device_id_type=MESH)
+        return carry
+
+    def greet_plane(o, carry):
+        pl.semaphore_signal(barrier, inc=1, device_id=plane(o), device_id_type=MESH)
         return carry
 
     def greet_z(o, carry):
         pl.semaphore_signal(barrier, inc=1, device_id=along_z(o), device_id_type=MESH)
         return carry
 
-    lax.fori_loop(1, 32, greet_ctx, 0)
+    lax.fori_loop(0, 16, greet_far, 0)
     lax.fori_loop(1, 8, greet_z, 0)
     lax.fori_loop(9, 16, greet_z, 0)
+    lax.fori_loop(1, 16, greet_plane, 0)
     for axis, offset in [(0, 0), (0, 1), (0, 2), (0, 3), (1, 1), (1, 2), (1, 3)]:
         pl.semaphore_signal(barrier, inc=1, device_id=line(axis, offset, 1), device_id_type=MESH)
     loads = [
@@ -121,9 +116,11 @@
 
     halves = [pl.ds(0, HD), pl.ds(HD, HD)]
     kz = [remote(kv.at[:, half], kvb.at[SEEN, :, half], kz_s.at[i], kz_r.at[i], partner) for i, half in enumerate(halves)]
-    launch(*kz)
-    kp = [remote(kv, kvb.at[o], kp_s.at[o - 1], kp_r.at[o - 1], plane(o)) for o in range(1, SEEN)]
-    launch(*kp)
+    for cp in kz:
+        start([cp], cp)
+    kp = [remote(kv, kvb.at[o], kp_s, kp_r, plane(o)) for o in range(1, SEEN)]
+    kp_whole = whole(kvb.at[pl.ds(0, SEEN - 1)], kp_s, kp_r)
+    start(kp, kp_whole)
 
     loads[3].wait()
 
@@ -150,12 +147,10 @@
     x_copies = {}
     for axis in range(2):
         for offset, flip in OTHERS:
-            m = axis * 7 + offset * 2 + flip - 1
-            x_copies[axis, offset, flip] = remote(x_source(axis, offset, flip), x_place(axis), x_s.at[m], x_r.at[m], line(axis, offset, flip))
+            x_copies[axis, offset, flip] = remote(x_source(axis, offset, flip), x_place(axis), x_s.at[axis], x_r.at[axis], line(axis, offset, flip))
     x_own = [pltpu.make_async_copy(x_source(axis, 0, 0), x_place(axis), loc_sem.at[7 + axis]) for axis in range(2)]
     for cp in x_own:
         cp.start()
-    launch(*[cp for (axis, offset, flip), cp in x_copies.items() if offset != 2])
 
     for cp in loads[4:]:
         cp.wait()
@@ -188,11 +183,75 @@
 
     kf = []
     for i, half in enumerate(halves):
-        take(kz[i])
-        for o in range(1, SEEN):
-            cp = remote(kvb.at[SEEN, :, half], kvb.at[SEEN + o, :, half], kf_s.at[i * 4 + o - 1], kf_r.at[i * 4 + o - 1], plane(o))
-            launch(cp)
-            kf.append(cp)
+        kz[i].wait_recv()
+        cps = [remote(kvb.at[SEEN, :, half], kvb.at[SEEN + o, :, half], kf_s.at[i], kf_r.at[i], plane(o)) for o in range(1, SEEN)]
+        kf.append(whole(kvb.at[pl.ds(0, SEEN - 1), :, half], kf_s.at[i], kf_r.at[i]))
+        start(cps, kf[i])
+    for (axis, offset, flip), cp in x_copies.items():
+        if offset != 2:
+            cp.start()
+
+    half_rows = SEEN * T
+
+    def scores_of(rel):
+        at = pl.ds(rel * half_rows, half_rows)
+        keys = kvb[pl.ds(rel * SEEN, SEEN), :, :HD].reshape(half_rows, HD)
+        values = kvb[pl.ds(rel * SEEN, SEEN), :, HD:].reshape(half_rows, HD)
+        for h in range(HQ):
+            heads = pl.ds(h * T, T)
+            score[at, heads] = dot_nt(keys, q_st[heads, :]) * SCALE + bias[at, :]
+            grad_prob[at, heads] = dot_nt(values, o_st[heads, :])
+
+    loads[2].wait()
+    kp_whole.wait_recv()
+    scores_of(0)
+    for group in kf:
+        group.wait_recv()
+    scores_of(1)
+    for h in range(HQ):
+        heads = pl.ds(h * T, T)
+        scores = score[:, heads]
+        weights = jnp.exp(scores - jnp.max(scores, axis=0, keepdims=True))
+        probs = weights * (1.0 / jnp.sum(weights, axis=0, keepdims=True))
+        row_dot = jnp.sum(probs * grad_prob[:, heads], axis=0, keepdims=True)
+        ds_st[:, heads] = (probs * (grad_prob[:, heads] - row_dot)).astype(jnp.bfloat16)
+        p_st[:, heads] = probs.astype(jnp.bfloat16)
+
+    def term(rel, half):
+        at = pl.ds(rel * half_rows, half_rows)
+        if half == VALUE:
+            return dot_nn(p_st[at, :], o_st[...])
+        return dot_nn(ds_st[at, :], q_st[...]) * SCALE
+
+    sent = {}
+    for rel in (1, 0):
+        for half in (VALUE, KEY):
+            terms = term(rel, half)
+            own_far[half, rel] = terms[:T]
+            part[half, pl.ds(rel * 4, 4)] = terms[T:].astype(jnp.bfloat16).reshape(SEEN - 1, T, HD)
+            at = pl.ds(rel * 4, 4)
+            send, recv = d_s.at[half, rel], d_r.at[half, rel]
+            cps = [remote(part.at[half, rel * 4 + o - 1], got.at[half, rel * 4 + o - 1], send, recv, plane(16 - o)) for o in range(1, SEEN)]
+            sent[rel, half] = whole(got.at[half, at], send, recv)
+            start(cps, sent[rel, half])
+
+    def terms_sum(rel, half):
+        sent[rel, half].wait_recv()
+        total = own_far[half, rel]
+        for o in range(SEEN - 1):
+            total = total + got[half, rel * 4 + o].astype(jnp.float32)
+        return total
+
+    dz = []
+    for half in (VALUE, KEY):
+        far_sum[half] = terms_sum(1, half).astype(jnp.bfloat16)
+        dz.append(remote(far_sum.at[half], far_got.at[half], dz_s.at[half], dz_r.at[half], partner))
+        start([dz[half]], dz[half])
+    for (axis, offset, flip), cp in x_copies.items():
+        if offset == 2:
+            cp.start()
+    x_whole = [whole(x_all.at[axis, :, :, pl.ds(0, 7 * T)], x_s.at[axis], x_r.at[axis]) for axis in range(2)]
+    sends.extend(x_whole)
     plan_row = plan[pl.ds(c, 1), :]
     out_row = lax.broadcasted_iota(jnp.int32, (4 * T, 32), 0)
     span_no = lax.broadcasted_iota(jnp.int32, (4 * T, 32), 1)
@@ -203,111 +262,60 @@
         col_no = lax.broadcasted_iota(jnp.int32, (4 * T, T), 1) + h * T
         onehot[:, pl.ds(h * T, T)] = jnp.where(col_no == source, 1.0, 0.0).astype(jnp.bfloat16)
 
-    loads[2].wait()
-    take(*kp)
-    take(*kf)
-
-    n_keys = 2 * SEEN * T
-    keys = kvb[:, :, :HD].reshape(n_keys, HD)
-    values = kvb[:, :, HD:].reshape(n_keys, HD)
+
     for s in range(2 * SEEN):
         k_t[:, pl.ds(s * T, T)] = kvb[s, :, :HD].T
-    for h in range(HQ):
-        heads = pl.ds(h * T, T)
-        scores = dot_nt(keys, q_st[heads, :]) * SCALE + bias[...]
-        top = jnp.max(scores, axis=0, keepdims=True)
-        weights = jnp.exp(scores - top)
-        probs = weights * (1.0 / jnp.sum(weights, axis=0, keepdims=True))
-        grad_prob = dot_nt(values, o_st[heads, :])
-        row_dot = jnp.sum(probs * grad_prob, axis=0, keepdims=True)
-        ds_st[:, heads] = (probs * (grad_prob - row_dot)).astype(jnp.bfloat16)
-        p_st[:, heads] = probs.astype(jnp.bfloat16)
-
-    half_rows = SEEN * T
-
-    def term(rel, half):
-        at = pl.ds(rel * half_rows, half_rows)
-        if half == VALUE:
-            return dot_nn(p_st[at, :], o_st[...])
-        return dot_nn(ds_st[at, :], q_st[...]) * SCALE
-
-    sent = {}
-    for rel in (1, 0):
-        for half in (VALUE, KEY):
-            terms = term(rel, half)
-            own_far[half, rel] = terms[:T]
-            part[half, pl.ds(rel * 4, 4)] = terms[T:].astype(jnp.bfloat16).reshape(SEEN - 1, T, HD)
-            sent[rel, half] = []
-            for o in range(1, SEEN):
-                i = rel * 4 + o - 1
-                cp = remote(part.at[half, i], got.at[half, i], d_s.at[half, i], d_r.at[half, i], plane(16 - o))
-                launch(cp)
-                sent[rel, half].append(cp)
-
     q_grad_t = (dot_nn(k_t[...], ds_st[...]) * SCALE).astype(jnp.bfloat16)
     q_send[...] = dot_nt(onehot[...], q_grad_t).astype(jnp.bfloat16).reshape(32, 16, HD)
     q_recv[c] = q_send[c]
 
-    def terms_sum(rel, half):
-        take(*sent[rel, half])
-        total = own_far[half, rel]
-        for o in range(SEEN - 1):
-            total = total + got[half, rel * 4 + o].astype(jnp.float32)
-        return total
-
-    dz = []
-    for half in (VALUE, KEY):
-        far_sum[half] = terms_sum(1, half).astype(jnp.bfloat16)
-        dz.append(remote(far_sum.at[half], far_got.at[half], dz_s.at[half], dz_r.at[half], partner))
-        launch(dz[half])
-    launch(*[cp for (axis, offset, flip), cp in x_copies.items() if offset == 2])
     def q_copy(o):
         there = lax.rem(c + o, 32)
-        return remote(q_send.at[there], q_recv.at[c], qa_s.at[o - 1], qa_r.at[o - 1], (d, there))
-
-    launch_all(q_copy, 1, 32)
+        return remote(q_send.at[there], q_recv.at[c], qa_s, qa_r, (d, there))
+
+    q_whole = whole(q_recv.at[pl.ds(0, 31)], qa_s, qa_r)
+
+    start_all(q_copy, 1, 32)
+    sends.append(q_whole)
 
     near = [terms_sum(0, half) for half in (VALUE, KEY)]
 
     g_copies = {}
     for half in (VALUE, KEY):
-        take(dz[half])
+        dz[half].wait_recv()
         kvg = (near[half] + far_got[half].astype(jnp.float32)).astype(jnp.bfloat16)
         kvg_out[:, COLUMNS[half]] = kvg
         for axis in range(2):
             g_all[half, axis, own_slot[axis]] = kvg
         for axis in range(2):
-            g_copies[half, axis] = []
-            for offset, flip in OTHERS:
-                m = axis * 7 + offset * 2 + flip - 1
-                slot = g_all.at[half, axis, own_slot[axis]]
-                cp = remote(slot, slot, g_s.at[half, m], g_r.at[half, m], line(axis, offset, flip))
-                launch(cp)
-                g_copies[half, axis].append(cp)
-
-    take(*x_copies.values())
-    for cp in x_own:
-        cp.wait()
+            slot = g_all.at[half, axis, own_slot[axis]]
+            send, recv = g_s.at[half, axis], g_r.at[half, axis]
+            g_copies[half, axis] = whole(g_all.at[half, axis, pl.ds(0, 7)], send, recv)
+            start([remote(slot, slot, send, recv, line(axis, offset, flip)) for offset, flip in OTHERS], g_copies[half, axis])
+
+    for axis in range(2):
+        x_whole[axis].wait_recv()
+        x_own[axis].wait()
 
     w_copies = {}
     for half in (VALUE, KEY):
         for axis in range(2):
-            take(*g_copies[half, axis])
+            g_copies[half, axis].wait_recv()
             terms = dot_nn(x_all[axis].reshape(4 * T, 8 * T), g_all[half, axis].reshape(8 * T, HD)).reshape(4, T, HD)
             w_acc[half, axis] = terms
             w_send[half, axis] = terms.astype(jnp.bfloat16)
-            w_copies[half, axis] = []
+            send, recv = w_s.at[half, axis], w_r.at[half, axis]
+            cps = []
             for offset in (2, 1, 3):
-                m = axis * 3 + offset - 1
                 there = lax.rem(own_pos[1 - axis] + offset, 4)
-                cp = remote(w_send.at[half, axis, there], w_got.at[half, m], w_s.at[half, m], w_r.at[half, m], line(1 - axis, offset, 0))
-                launch(cp)
-                w_copies[half, axis].append(cp)
+                cps.append(remote(w_send.at[half, axis, there], w_got.at[half, axis * 3 + offset - 1], send, recv, line(1 - axis, offset, 0)))
+            w_copies[half, axis] = whole(w_got.at[half, pl.ds(axis * 3, 3)], send, recv)
+            start(cps, w_copies[half, axis])
 
     z_copies = []
     for half in (VALUE, KEY):
         for axis in range(2):
-            take(*w_copies[half, axis])
+            w_copies[half, axis].wait_recv()
             total = w_acc[half, axis, own_pos[1 - axis]]
             for offset in range(1, 4):
                 total = total + w_got[half, axis * 3 + offset - 1].astype(jnp.float32)
@@ -315,12 +323,12 @@
         w_z_got[half, z] = w_z[half, z]
 
         def z_copy(o, half=half):
-            return remote(w_z.at[half, lax.rem(z + o, 16)], w_z_got.at[half, z], z_s.at[half, o - 1], z_r.at[half, o - 1], along_z(o))
-
-        launch_all(z_copy, 1, 16)
-        z_copies.append(z_copy)
-
-    take_all(q_copy, 1, 32)
+            return remote(w_z.at[half, lax.rem(z + o, 16)], w_z_got.at[half, z], z_s.at[half], z_r.at[half], along_z(o))
+
+        start_all(z_copy, 1, 16)
+        z_copies.append(whole(w_z_got.at[half, pl.ds(0, 15)], z_s.at[half], z_r.at[half]))
+
+    q_whole.wait_recv()
     arrived = q_recv[...].reshape(4 * T, HD)
     tok = lax.broadcasted_iota(jnp.int32, (T, 4 * T), 0)
     place = lax.broadcasted_iota(jnp.int32, (T, 4 * T), 1)
@@ -328,22 +336,13 @@
         pick = jnp.where(place == tok // 4 * 16 + h * 4 + tok % 4, 1.0, 0.0).astype(jnp.bfloat16)
         qg_out[:, pl.ds(h * HD, HD)] = dot_nn(pick, arrived).astype(jnp.bfloat16)
 
+    drain(sends)
     for half in (VALUE, KEY):
-        take_all(z_copies[half], 1, 16)
+        z_copies[half].wait_recv()
         total = jnp.sum(w_z_got[half].astype(jnp.float32), axis=0)
         wg_out[:, COLUMNS[half]] = (total * (1.0 / 256.0)).astype(jnp.bfloat16)
-
-    for item in sends:
-        if isinstance(item, tuple):
-            make, low, high = item
-
-            def step(o, carry, make=make):
-                make(o).wait_send()
-                return carry
-
-            lax.fori_loop(low, high, step, 0)
-        else:
-            item.wait_send()
+    drain(z_copies)
+
 
 def local(normed, query, key_value, output_grad, lengths, advantage, span_plan):
     bf16, f32 = jnp.bfloat16, jnp.float32
@@ -370,6 +369,8 @@
             pltpu.VMEM((2 * SEEN, T, 2 * HD), bf16),
             pltpu.VMEM((HD, n_keys), bf16),
             pltpu.VMEM((n_keys, T), f32),
+            pltpu.VMEM((n_keys, HQ * T), f32),
+            pltpu.VMEM((n_keys, HQ * T), f32),
             pltpu.VMEM((n_keys, HQ * T), bf16),
             pltpu.VMEM((n_keys, HQ * T), bf16),
             pltpu.VMEM((HQ * T, HQ * T), bf16),
@@ -389,9 +390,9 @@
             pltpu.VMEM((2, 6, T, HD), bf16),
             pltpu.VMEM((2, 16, 16, HD), bf16),
             pltpu.VMEM((2, 16, 16, HD), bf16),
-            dma((9,)), dma((2,)), dma((2,)), dma((4,)), dma((4,)), dma((8,)), dma((8,)),
-            dma((14,)), dma((14,)), dma((2, 8)), dma((2, 8)), dma((2,)), dma((2,)), dma((31,)), dma((31,)),
-            dma((2, 14)), dma((2, 14)), dma((2, 6)), dma((2, 6)), dma((2, 15)), dma((2, 15)),
+            dma((9,)), dma((2,)), dma((2,)), dma, dma, dma((2,)), dma((2,)),
+            dma((2,)), dma((2,)), dma((2, 2)), dma((2, 2)), dma((2,)), dma((2,)), dma, dma,
+            dma((2, 2)), dma((2, 2)), dma((2, 2)), dma((2, 2)), dma((2,)), dma((2,)),
         ],
         compiler_params=pltpu.CompilerParams(collective_id=0, has_side_effects=True, vmem_limit_bytes=48 * 2**20),
         name="backward",

time: 83.7 us -> 78.6 us (0.939)
  Pallas kernels: 81 us -> 76 us
    pallas_call x1, Pallas kernels: 81 us -> 76 us  [local(): pl.pallas_call(kernel, out_shape=(jax.ShapeDtypeStruct((T, HQ * HD), bf16...]
where the time goes in v4:
time: 78.6 us; the launch traced here: 78.5 us
  Pallas kernels  76 us (97%)
  local copies, waits for them, and re-layouts  1.88 us (2%)
    pallas_call x1, Pallas kernels, local(): pl.pallas_call(kernel, out_shape=(jax.ShapeDtypeStruct((T, HQ * HD), bf16...  76 us
    unnamed x3, local copies, waits for them, and re-layouts  1.88 us

profile of v4, /device:TPU:1, one launch (start us, length us, event | category | flops | bytes accessed | tf_op | source)
XLA Modules:
  0.0 78.5 jit_solution(4846305307805419087)
XLA Ops:
  0.6 76.0 %backward.1 = (bf16[128,512]{1,0:T(8,128)(2,1)S(1)}, bf16[128,256]{1,0:T(8,128)(2,1)S(1)}, bf16[16,256]{1,0:T(8,128)(2,1)S(1)}) custom-call(bf16[128,8192]{1,0:T(8,128)(2,1)} %normed.1, bf16[128,512]{1,0:T(8,128)(2,1)} %query.1, bf16[128,256]{1,0:T(8,128)(2,1)} %kv.1, bf16[128,512]{1,0:T(8,128)(2,1)} %og.1, s32[1,16]{1,0:T(1,128)} %lengths_in.1, ...), custom_call_target="tpu_custom_call" | custom-call | tf_op jit(solution)/shard_map/backward/pallas_call | solution.py:352
  76.6 0.7 copy.13
  77.3 0.6 copy.14
  77.9 0.6 copy.15

commit v5 on v4

--- a/solution.py
+++ b/solution.py
@@ -69,11 +69,8 @@
         sends.append(group)
 
     def start_all(make, low, high):
-        def step(o, carry):
+        for o in range(low, high):
             make(o).start()
-            return carry
-
-        lax.fori_loop(low, high, step, 0)
 
     def drain(items):
         for cp in items:
@@ -81,23 +78,16 @@
 
     barrier = pltpu.get_barrier_semaphore()
 
-    def greet_far(o, carry):
-        there = lax.rem(j + o, 16) * 2 + (1 - p)
-        pl.semaphore_signal(barrier, inc=1, device_id=(d, there), device_id_type=MESH)
-        return carry
-
-    def greet_plane(o, carry):
-        pl.semaphore_signal(barrier, inc=1, device_id=plane(o), device_id_type=MESH)
-        return carry
-
-    def greet_z(o, carry):
-        pl.semaphore_signal(barrier, inc=1, device_id=along_z(o), device_id_type=MESH)
-        return carry
-
-    lax.fori_loop(0, 16, greet_far, 0)
-    lax.fori_loop(1, 8, greet_z, 0)
-    lax.fori_loop(9, 16, greet_z, 0)
-    lax.fori_loop(1, 16, greet_plane, 0)
+    def greet(where):
+        pl.semaphore_signal(barrier, inc=1, device_id=where, device_id_type=MESH)
+
+    for o in range(16):
+        greet((d, lax.rem(j + o, 16) * 2 + (1 - p)))
+    for o in range(1, 16):
+        if o != 8:
+            greet(along_z(o))
+    for o in range(1, 16):
+        greet(plane(o))
     for axis, offset in [(0, 0), (0, 1), (0, 2), (0, 3), (1, 1), (1, 2), (1, 3)]:
         pl.semaphore_signal(barrier, inc=1, device_id=line(axis, offset, 1), device_id_type=MESH)
     loads = [

time: 78.6 us -> 78.3 us (level)
  no operation moved by 1% of the time
where the time goes in v5:
time: 78.3 us; the launch traced here: 78.2 us
  Pallas kernels  75.6 us (97%)
  local copies, waits for them, and re-layouts  1.88 us (2%)
    pallas_call x1, Pallas kernels, local(): pl.pallas_call(kernel, out_shape=(jax.ShapeDtypeStruct((T, HQ * HD), bf16...  75.6 us
    unnamed x3, local copies, waits for them, and re-layouts  1.88 us

profile of v5, /device:TPU:1, one launch (start us, length us, event | category | flops | bytes accessed | tf_op | source)
XLA Modules:
  0.0 78.2 jit_solution(943019083862597599)
XLA Ops:
  0.6 75.6 %backward.1 = (bf16[128,512]{1,0:T(8,128)(2,1)S(1)}, bf16[128,256]{1,0:T(8,128)(2,1)S(1)}, bf16[16,256]{1,0:T(8,128)(2,1)S(1)}) custom-call(bf16[128,8192]{1,0:T(8,128)(2,1)} %normed.1, bf16[128,512]{1,0:T(8,128)(2,1)} %query.1, bf16[128,256]{1,0:T(8,128)(2,1)} %kv.1, bf16[128,512]{1,0:T(8,128)(2,1)} %og.1, s32[1,16]{1,0:T(1,128)} %lengths_in.1, ...), custom_call_target="tpu_custom_call" | custom-call | tf_op jit(solution)/shard_map/backward/pallas_call | solution.py:342
  76.3 0.7 copy.13
  76.9 0.6 copy.14
  77.6 0.6 copy.15

commit v6 on v5

--- a/solution.py
+++ b/solution.py
@@ -315,7 +315,8 @@
         def z_copy(o, half=half):
             return remote(w_z.at[half, lax.rem(z + o, 16)], w_z_got.at[half, z], z_s.at[half], z_r.at[half], along_z(o))
 
-        start_all(z_copy, 1, 16)
+        for o in sorted(range(1, 16), key=lambda o: -min(o, 16 - o)):
+            z_copy(o).start()
         z_copies.append(whole(w_z_got.at[half, pl.ds(0, 15)], z_s.at[half], z_r.at[half]))
 
     q_whole.wait_recv()

time: 78.3 us -> 78.2 us (level)
  no operation moved by 1% of the time
where the time goes in v6:
time: 78.2 us; the launch traced here: 78.1 us
  Pallas kernels  75.6 us (97%)
  local copies, waits for them, and re-layouts  1.88 us (2%)
    pallas_call x1, Pallas kernels, local(): pl.pallas_call(kernel, out_shape=(jax.ShapeDtypeStruct((T, HQ * HD), bf16...  75.6 us
    unnamed x3, local copies, waits for them, and re-layouts  1.88 us

profile of v6, /device:TPU:1, one launch (start us, length us, event | category | flops | bytes accessed | tf_op | source)
XLA Modules:
  0.0 78.1 jit_solution(1017459813454566757)
XLA Ops:
  0.6 75.6 %backward.1 = (bf16[128,512]{1,0:T(8,128)(2,1)S(1)}, bf16[128,256]{1,0:T(8,128)(2,1)S(1)}, bf16[16,256]{1,0:T(8,128)(2,1)S(1)}) custom-call(bf16[128,8192]{1,0:T(8,128)(2,1)} %normed.1, bf16[128,512]{1,0:T(8,128)(2,1)} %query.1, bf16[128,256]{1,0:T(8,128)(2,1)} %kv.1, bf16[128,512]{1,0:T(8,128)(2,1)} %og.1, s32[1,16]{1,0:T(1,128)} %lengths_in.1, ...), custom_call_target="tpu_custom_call" | custom-call | tf_op jit(solution)/shard_map/backward/pallas_call | solution.py:343
  76.2 0.7 copy.13
  76.9 0.6 copy.14
  77.5 0.6 copy.15
